TPU v7x, 128 devices: a whole 4x4x4 slice. The times are simulated.
128 devices in a mesh: slab: 16 (over z, x_lo, core), head: 8 (over x_hi, y).
Axes of the slice: x: 4 (x_hi: 2, x_lo: 2; x = x_hi * 2 + x_lo), y: 4, z: 4, core: 2. Of those that a mesh axis runs over, the one named last changes fastest.
Arguments:
- hidden: bfloat16 [12288, 3072], P('slab', 'head'), may hold values from -48 to 48
- w_qkv: bfloat16 [3072, 3, 3072], P(None, None, 'head'), may hold values from -0.109375 to 0.109375
- text_keys: bfloat16 [2, 256, 3072], P(None, None, 'head'), may hold values from -6 to 6
- text_values: bfloat16 [2, 256, 3072], P(None, None, 'head'), may hold values from -6 to 6
- text_len: int32 [2], replicated, may hold values from 64 to 256, as said below
- advantage: float32 [2], replicated, may hold values from -2 to 2
- out_grad: bfloat16 [12288, 3072], P('slab', 'head'), may hold values from -6 to 6
- tile_lists: int32 [32, 3], P('slab'), may hold values from -1 to 31, as said below
Outputs:
- hidden_grad: bfloat16 [12288, 3072], P('slab', 'head')
- weight_grad: bfloat16 [3072, 3, 3072], P('slab', None, 'head')
- text_grad: bfloat16 [2, 256, 2, 3072], P(None, None, None, 'head')
Inputs may be any that keep to these rules, and one draw needn't show every extreme that they name: `tile_lists`: tiles lie on a grid of (16) time layers by 2 samples by 1 tiles, numbered time, sample, width from slowest. Row i lists, in random order, itself, every tile of the same sample and time layer within one step in width, and some of the tiles of the same sample within one step in time and width, followed by -1 in the remaining slots; j is in row i exactly when i is in row j. `text_len`: some sample has all 256 text tokens live.
All inputs are finite; a program needn't handle non-finite values.
Results may differ from a plain program's by a relative error of at most 0.014.
The roundings to bfloat16 on the way count: a program that leaves them out, or rounds other values in their place, can miss the bound.
Values may be sent and summed in bfloat16 or wider, within the bound.
No kernel may reach another device: no remote copies, remote signals or barrier semaphores. Data moves between devices by JAX's collectives and lax.ppermute only.
A program may use at most 128 MiB of HBM per device.

v0:
```python
import math

import jax
import jax.numpy as jnp
from jax import lax
from jax.sharding import PartitionSpec as P

DH = 128
TILE = 384
SAMPLES = 2


def with_halo(value, sides, width):
    for axis, dim in sides:
        devices, length = (lax.axis_size(axis), value.shape[dim])
        up = [(i, (i + 1) % devices) for i in range(devices - 1)]
        down = [(j, i) for i, j in up]
        last = lax.slice_in_dim(value, length - width, length, axis=dim)
        leading = lax.slice_in_dim(value, 0, width, axis=dim)
        before = lax.ppermute(last, axis, up)
        after = lax.ppermute(leading, axis, down)
        value = jnp.concatenate([before, value, after], axis=dim)
    return value


def from_behind(block, axis, distance):
    devices = range(lax.axis_size(axis))
    route = [(i - distance, i) for i in devices if i - distance in devices]
    return lax.ppermute(block, axis, route)


def forward_part(query_rows, cot_rows, keys, vals, key_mask, scale):
    scores = (
        jnp.einsum("qhd,khd->hqk", query_rows, keys, preferred_element_type=jnp.float32) * scale
    )
    scores = jnp.where(key_mask[None, None, :], scores, -jnp.inf)
    top = jnp.max(scores, axis=2, keepdims=True)
    lse = top + jnp.log(jnp.sum(jnp.exp(scores - top), axis=2, keepdims=True))
    probs = jnp.exp(scores - lse)
    probs_b = probs.astype(jnp.bfloat16)
    attn = jnp.einsum("hqk,khd->qhd", probs_b, vals, preferred_element_type=jnp.float32)
    delta = jnp.sum(cot_rows.astype(jnp.float32) * attn, axis=2).T
    dprobs = jnp.einsum("qhd,khd->hqk", cot_rows, vals, preferred_element_type=jnp.float32)
    dscores = (probs * (dprobs - delta[:, :, None]) * scale).astype(jnp.bfloat16)
    query_grad = jnp.einsum("hqk,khd->qhd", dscores, keys, preferred_element_type=jnp.float32)
    return (probs_b, dscores, query_grad, lse[:, :, 0], delta)


def weight_maker(full_hidden, parts):
    return jnp.einsum("td,tch->dch", full_hidden, parts, preferred_element_type=jnp.float32)


def body(hidden, w_qkv, text_keys, text_values, text_len, advantage, out_grad, tile_lists):
    tokens_dev = hidden.shape[0]
    tiles_dev = tokens_dev // TILE
    group = tiles_dev // SAMPLES
    width = w_qkv.shape[2]
    heads_dev = width // DH
    scale = 1.0 / math.sqrt(DH)
    slab_index = lax.axis_index("slab")
    slots_count = tile_lists.shape[1]
    nvid = slots_count * TILE
    full_hidden = lax.all_gather(hidden, "head", axis=1, tiled=True)
    proj = jnp.einsum("td,dch->tch", full_hidden, w_qkv, preferred_element_type=jnp.float32).astype(
        jnp.bfloat16
    )
    query_rows = proj[:, 0]
    key_rows = proj[:, 1]
    value_rows = proj[:, 2]
    tile_owner = jnp.arange(tiles_dev, dtype=jnp.int32) // group
    owner_match = tile_owner[:, None] == jnp.arange(SAMPLES, dtype=jnp.int32)[None, :]
    adv_tiles = jnp.sum(jnp.where(owner_match, advantage[None, :], 0.0), axis=1)
    out_cot = adv_tiles[:, None, None] * out_grad.astype(jnp.float32).reshape(
        tiles_dev, TILE, width
    )
    out_cot = out_cot.reshape(tokens_dev, width).astype(jnp.bfloat16)
    text_k_all = text_keys.reshape(SAMPLES, -1, heads_dev, DH)
    text_v_all = text_values.reshape(SAMPLES, -1, heads_dev, DH)
    text_rows = text_k_all.shape[1]
    usable = tile_lists >= 0
    local = jnp.where(usable, tile_lists - (slab_index - 1) * tiles_dev, 0)
    query_tiles = query_rows.reshape(tiles_dev, TILE, heads_dev, DH)
    cot_tiles = out_cot.reshape(tiles_dev, TILE, heads_dev, DH)
    kv_local = jnp.concatenate([key_rows, value_rows], axis=1)
    kv_buffer = with_halo(kv_local, (("slab", 0),), tokens_dev)
    kv_tiles = kv_buffer.reshape(3 * tiles_dev, TILE, 2 * width)

    def own_tile(index):
        listed = local[index]
        live = usable[index]
        owner = index // group
        text_k = lax.dynamic_index_in_dim(text_k_all, owner, 0, keepdims=False)
        text_v = lax.dynamic_index_in_dim(text_v_all, owner, 0, keepdims=False)
        text_count = lax.dynamic_index_in_dim(text_len, owner, 0, keepdims=False)
        text_mask = jnp.arange(text_rows, dtype=jnp.int32) < text_count
        chosen = kv_tiles[listed]
        video_k = chosen[:, :, :width].reshape(nvid, heads_dev, DH)
        video_v = chosen[:, :, width:].reshape(nvid, heads_dev, DH)
        keys = jnp.concatenate([video_k, text_k], axis=0)
        vals = jnp.concatenate([video_v, text_v], axis=0)
        key_mask = jnp.concatenate([jnp.repeat(live, TILE), text_mask])
        query_here = query_tiles[index]
        cot_here = cot_tiles[index]
        probs_b, dscores, query_grad, lse, delta = forward_part(
            query_here, cot_here, keys, vals, key_mask, scale
        )
        key_part = jnp.einsum(
            "hqk,qhd->khd", dscores, query_here, preferred_element_type=jnp.float32
        )
        value_part = jnp.einsum(
            "hqk,qhd->khd", probs_b, cot_here, preferred_element_type=jnp.float32
        )
        video = jnp.concatenate(
            [key_part[:nvid].reshape(nvid, width), value_part[:nvid].reshape(nvid, width)], axis=1
        )
        text_part = jnp.concatenate(
            [key_part[nvid:].reshape(-1, width), value_part[nvid:].reshape(-1, width)], axis=1
        )
        extra = video.reshape(slots_count, TILE, 2 * width)
        return (query_grad.reshape(TILE, width).astype(jnp.bfloat16), extra, text_part)

    tile_ids = jnp.arange(tiles_dev, dtype=jnp.int32)
    query_grads, video_terms, text_terms = lax.map(lambda index: own_tile(index), tile_ids)
    query_flat = query_grads.reshape(tokens_dev, 1, width)
    flat_terms = video_terms.reshape(tiles_dev * slots_count, TILE * 2 * width)
    targets = jnp.arange(3 * tiles_dev, dtype=jnp.int32)
    onehot = (
        (local.reshape(-1)[None, :] == targets[:, None]) & usable.reshape(-1)[None, :]
    ).astype(jnp.float32)
    collected = jnp.dot(
        onehot, flat_terms, precision=lax.Precision.HIGHEST, preferred_element_type=jnp.float32
    )
    lower = collected[:tiles_dev]
    upper = collected[2 * tiles_dev :]
    from_above = from_behind(lower, "slab", -1)
    from_below = from_behind(upper, "slab", 1)
    key_sums = (collected[tiles_dev : 2 * tiles_dev] + from_above + from_below).reshape(
        tokens_dev, 2 * width
    )
    key_grad = key_sums[:, :width].astype(jnp.bfloat16)
    value_grad = key_sums[:, width:].astype(jnp.bfloat16)
    kv_grads = jnp.stack([key_grad, value_grad], axis=1)
    grads = jnp.concatenate([query_flat, kv_grads], axis=1)
    text_total = jnp.sum(text_terms.reshape(SAMPLES, group, text_rows, 2 * width), axis=1)
    text_sums = lax.psum(text_total, "slab")
    text_grad = text_sums.reshape(SAMPLES, -1, 2, width).astype(jnp.bfloat16)
    input_term = jnp.einsum("tch,dch->td", grads, w_qkv, preferred_element_type=jnp.float32)
    hidden_grad = lax.psum_scatter(input_term, "head", scatter_dimension=1, tiled=True).astype(
        jnp.bfloat16
    )
    weight_grad = lax.psum_scatter(
        weight_maker(full_hidden, grads), "slab", scatter_dimension=0, tiled=True
    ).astype(jnp.bfloat16)
    return (hidden_grad, weight_grad, text_grad)


def solution(mesh):
    in_specs = (
        P("slab", "head"),
        P(None, None, "head"),
        P(None, None, "head"),
        P(None, None, "head"),
        P(),
        P(),
        P("slab", "head"),
        P("slab", None),
    )
    out_specs = (P("slab", "head"), P("slab", None, "head"), P(None, None, None, "head"))
    return jax.shard_map(body, mesh=mesh, in_specs=in_specs, out_specs=out_specs, check_vma=False)
```

profile of v0, /device:TPU:1, one launch (start us, length us, event | category | flops | bytes accessed | tf_op | source)
XLA Modules:
  0.0 620.0 jit_solution(1655362361225788390)
XLA Ops:
  7.9 83.6 %all-gather.2.cloned.1.call-done = bf16[768,3072]{1,0:T(8,128)(2,1)} async-done(((bf16[768,384]{1,0:T(8,128)(2,1)}), bf16[768,3072]{1,0:T(8,128)(2,1)}) %all-gather.2.cloned.1.call-update) | async-done | bytes 4718608 | tf_op jit(solution)/shard_map/all_gather | solution.py:63
  91.5 10.3 %fusion.31 = bf16[768,3,384]{0,2,1:T(8,128)(2,1)S(1)} fusion(bf16[3072,3,384]{2,0,1:T(8,128)(2,1)} %param.11, bf16[768,3072]{1,0:T(8,128)(2,1)} %all-gather.2.cloned.1.call-done), kind=kOutput, calls=%fused_computation.56 | convolution fusion | flops 5436702720 | bytes 13565952 | tf_op jit(solution)/shard_map/td,dch->tch/dot_general | solution.py:64
  102.8 1.1 pad_maximum_fusion.8
  103.9 3.0 collective-permute-start.1
  106.9 2.6 collective-permute-start
  111.1 0.9 copy.78
  112.0 1.0 copy.80
  113.5 0.9 copy.83
  114.6 1.8 copy.82
  116.4 14.5 %collective-permute-done.1 = bf16[768,768]{0,1:T(8,128)(2,1)S(1)} collective-permute-done((bf16[768,768]{0,1:T(8,128)(2,1)}, bf16[768,768]{0,1:T(8,128)(2,1)S(1)}, u32[]{:S(2)}, u32[]{:S(2)}) %collective-permute-start.1) | collective-permute-done | bytes 1179680 | tf_op jit(solution)/shard_map/ppermute | solution.py:21
  130.9 1.0 copy-done.10
  131.9 3.4 pad_maximum_fusion.6
  135.4 3.6 copy.77
  139.0 83.6 %while.16 = (s32[]{:T(128)}, bf16[2,384,384]{2,1,0:T(8,128)(2,1)}, f32[2,3,384,768]{3,2,1,0:T(8,128)}, f32[2,256,768]{1,2,0:T(8,128)}, s32[2]{0:T(128)S(1)}, /*i...) while((s32[]{:T(128)}, bf16[2,384,384]{2,1,0:T(8,128)(2,1)}, ...), condition=%wide.region_5.6_spmd, body=%wide.region_1.5_spmd.sunk | while | flops 2524447232 | bytes 128552088 | solution.py:123
  142.9 1.1 constant_dynamic-slice_fusion.5
  145.6 2.7 gather_fusion
  150.0 2.1 fusion.74
  152.1 1.1 exponential_reduce_fusion.2
  153.2 1.2 fusion.75
  154.4 2.0 multiply_convert_fusion.3
  156.4 2.6 convolution_bitcast_fusion.6
  159.0 1.9 convolution_convert_fusion.2
  162.1 1.0 copy-done
  163.2 1.5 slice-done.3
  164.7 2.3 reshape.182
  167.0 2.9 copy.122
  169.9 2.3 reshape.183
  172.2 4.1 copy.123
  176.2 1.0 fusion.76
  177.2 3.5 maximum_dynamic-update-slice_fusion.2
  184.6 1.1 constant_dynamic-slice_fusion.5
  187.3 2.7 gather_fusion
  191.7 2.1 fusion.74
  193.8 1.1 exponential_reduce_fusion.2
  194.9 1.2 fusion.75
  196.1 2.0 multiply_convert_fusion.3
  198.1 2.6 convolution_bitcast_fusion.6
  200.7 1.9 convolution_convert_fusion.2
  203.9 1.0 copy-done
  205.0 1.5 slice-done.3
  206.4 2.3 reshape.182
  208.7 2.9 copy.122
  211.6 2.3 reshape.183
  213.9 4.1 copy.123
  217.9 0.9 fusion.76
  218.8 3.6 maximum_dynamic-update-slice_fusion.2
  222.6 7.3 %copy.109 = f32[1,6,384,768]{3,1,2,0:T(8,128)S(1)} copy(f32[1,6,384,768]{3,2,1,0:T(8,128)} %bitcast.140) | data formatting | bytes 14155776
  229.9 5.1 fusion.35
  235.0 1.9 fusion.44
  236.9 1.9 collective-permute-start.2
  238.8 3.6 collective-permute-start.3
  242.5 44.5 %collective-permute-done.2 = f32[2,294912]{1,0:T(2,128)S(1)} collective-permute-done((f32[2,294912]{1,0:T(2,128)S(1)}, f32[2,294912]{1,0:T(2,128)S(1)}, u32[]{:S(2)}, u32[]{:S(2)}) %collective-permute-start.2) | collective-permute-done | bytes 2359328 | tf_op jit(solution)/shard_map/ppermute | solution.py:29
  287.0 2.5 fusion.30
  290.6 11.7 %convolution_bitcast_fusion.3 = f32[768,3072]{1,0:T(8,128)} fusion(bf16[3072,3,384]{2,0,1:T(8,128)(2,1)} %param.11, bf16[768,1,384]{2,0,1:T(8,128)(2,1)S(1)} %get-tuple-element.273, bf16[768,1,384]{2,0,1:T(8,128)(2,1)S(1)} %get-tuple-element.272, bf16[768,1,384]{2,0,1:T(8,128)(2,1)S(1)} %bitcast.147), kind=kOutput, calls=%fused_computation.46 | convolution fusion | flops 5437587456 | bytes 18284544 | tf_op jit(solution)/shard_map/tch,dch->td/dot_general | solution.py:147
  302.4 10.9 %fusion.25 = f32[3,384,3072]{2,1,0:T(8,128)} fusion(bf16[768,3072]{1,0:T(8,128)(2,1)} %all-gather.2.cloned.1.call-done, bf16[768,1,384]{2,0,1:T(8,128)(2,1)S(1)} %get-tuple-element.273, bf16[768,1,384]{2,0,1:T(8,128)(2,1)S(1)} %get-tuple-element.272, bf16[768,1,384]{2,0,1:T(8,128)(2,1)S(1)} %bitcast.148), kind=kOutput, calls=%fused_computation.47 | convolution fusion | flops 5437587456 | bytes 20643840 | tf_op jit(solution)/shard_map/td,tch->dch/dot_general | solution.py:50
  313.3 15.2 %copy.103 = f32[3072,1152]{1,0:T(8,128)} copy(f32[3072,1152]{0,1:T(8,128)} %bitcast.135) | data formatting | bytes 28311552
  328.5 1.4 copy-done.9
  329.9 89.1 %all-reduce.1 = bf16[2,256,768]{1,2,0:T(8,128)(2,1)S(1)} all-reduce(f32[2,256,768]{1,2,0:T(8,128)S(1)} %copy-done.9), channel_id=1, replica_groups=mesh['slab'=16,'head'=8] {'slab'}, use_global_device_ids=true, to_apply=%region_8.9 | all-reduce | flops 393216 | bytes 2359296 | tf_op jit(solution)/shard_map/psum | solution.py:145
  419.0 1.8 copy.100
  420.8 34.8 %reduce-scatter.5.cloned.1.call-done = f32[768,384]{1,0:T(8,128)} async-done(((f32[768,3072]{1,0:T(8,128)}), f32[768,384]{1,0:T(8,128)}) %reduce-scatter.5.cloned.1.call-update) | async-done | bytes 1179664 | tf_op jit(solution)/shard_map/reduce_scatter | solution.py:148
  455.6 2.1 convert_element_type.64
  457.7 152.9 %reduce-scatter.7.cloned.1.call-done = f32[192,1152]{1,0:T(8,128)} async-done(((f32[3072,1152]{1,0:T(8,128)}), f32[192,1152]{1,0:T(8,128)}) %reduce-scatter.7.cloned.1.call-update) | async-done | bytes 884752
  610.6 1.4 copy.104
  612.0 1.0 copy.88
  (145 shorter events, 18.3 us)
Async XLA Ops:
  7.2 84.4 %all-gather.2.cloned.1.call-start = ((), (), s32[]{:S(2)}) async-start(), calls=%async_computation.2 | async-start | bytes 5308416 | tf_op jit(solution)/shard_map/all_gather | solution.py:63
  7.9 447.7 %reduce-scatter.5.cloned.1.call-start = ((), (), s32[]{:S(2)}) async-start(), calls=%async_computation.3 | async-start | bytes 10616832 | tf_op jit(solution)/shard_map/reduce_scatter | solution.py:148
  101.8 7.7 %copy-start.17 = (s32[2,3]{1,0:T(2,128)S(1)}, s32[2,3]{1,0:T(2,128)}, u32[]{:S(2)}) copy-start(s32[2,3]{1,0:T(2,128)} %param.17) | copy-start | bytes 76
  101.9 9.0 %copy-start.20 = (f32[2]{0:T(128)S(1)}, f32[2]{0:T(128)}, u32[]{:S(2)}) copy-start(f32[2]{0:T(128)} %param.15) | copy-start | bytes 28
  101.9 9.2 %copy-start.15 = (bf16[2,256,384]{2,1,0:T(8,128)(2,1)S(1)}, bf16[2,256,384]{2,1,0:T(8,128)(2,1)}, u32[]{:S(2)}) copy-start(bf16[2,256,384]{2,1,0:T(8,128)(2,1)} %param.12) | copy-start | bytes 1179652
  102.0 0.8 copy-start.6
  102.0 1.9 copy-start.7
  102.0 10.0 %copy-start.16 = (bf16[2,256,384]{2,1,0:T(8,128)(2,1)S(1)}, bf16[2,256,384]{2,1,0:T(8,128)(2,1)}, u32[]{:S(2)}) copy-start(bf16[2,256,384]{2,1,0:T(8,128)(2,1)} %param.13) | copy-start | bytes 1179652
  102.0 10.9 %copy-start.14 = (bf16[768,384]{1,0:T(8,128)(2,1)S(1)}, bf16[768,384]{1,0:T(8,128)(2,1)}, u32[]{:S(2)}) copy-start(bf16[768,384]{1,0:T(8,128)(2,1)} %param.16) | copy-start | bytes 1769476
  103.9 27.0 %collective-permute-start.1 = (bf16[768,768]{0,1:T(8,128)(2,1)}, bf16[768,768]{0,1:T(8,128)(2,1)S(1)}, u32[]{:S(2)}, u32[]{:S(2)}) collective-permute-start(bf16[768,768]{0,1:T(8,128)(2,1)} %pad_maximum_fusion.8), channel_id=1, source_target_pairs={{8,0},{16,8},{24,16},{32,24},{40,32},{48,40},{56,48},{64,56},{72,6... | collective-permute-start | bytes 3538952 | tf_op jit(solution)/shard_map/ppermute | solution.py:21
  106.9 25.0 %collective-permute-start = (bf16[768,768]{0,1:T(8,128)(2,1)}, bf16[768,768]{0,1:T(8,128)(2,1)}, u32[]{:S(2)}, u32[]{:S(2)}) collective-permute-start(bf16[768,768]{0,1:T(8,128)(2,1)} %pad_maximum_fusion.8), channel_id=1, source_target_pairs={{0,8},{8,16},{16,24},{24,32},{32,40},{40,48},{48,56},{56,64},{64,7... | collective-permute-start | bytes 3538952 | tf_op jit(solution)/shard_map/ppermute | solution.py:20
  130.9 1.0 copy-start.10
  135.3 3.6 copy-start.21
  139.0 3.8 copy-start.22
  148.9 1.1 copy-start.4
  152.0 1.1 copy-start.1
  152.0 1.1 copy-start.2
  156.4 2.6 copy-start.8
  159.0 1.9 copy-start.5
  160.9 1.0 copy-start.3
  160.9 1.2 copy-start.11
  161.7 1.4 copy-start
  162.1 1.1 copy-start.12
  163.2 1.5 slice-start.3
  167.0 2.9 slice-start.1
  172.2 4.1 slice-start
  172.2 4.1 slice-start.2
  177.2 3.5 copy-start.23
  180.7 3.8 copy-start.22
  190.6 1.1 copy-start.4
  193.8 1.1 copy-start.1
  193.8 1.1 copy-start.2
  198.1 2.6 copy-start.8
  200.7 1.9 copy-start.5
  202.6 1.0 copy-start.3
  202.6 1.2 copy-start.11
  203.4 1.4 copy-start
  203.8 1.1 copy-start.12
  205.0 1.5 slice-start.3
  208.7 2.9 slice-start.1
  213.9 4.1 slice-start
  213.9 4.1 slice-start.2
  218.8 3.6 copy-start.23
  222.6 7.3 %copy-start.18 = (pred[6]{0:T(512)(128)(4,1)S(1)}, pred[6]{0:T(512)(128)(4,1)}, u32[]{:S(2)}) copy-start(pred[6]{0:T(512)(128)(4,1)} %and.22) | copy-start | bytes 22
  222.6 7.3 %copy-start.19 = (s32[6]{0:T(128)S(1)}, s32[6]{0:T(128)}, u32[]{:S(2)}) copy-start(s32[6]{0:T(128)} %eq.31) | copy-start | bytes 76
  236.9 50.1 %collective-permute-start.2 = (f32[2,294912]{1,0:T(2,128)S(1)}, f32[2,294912]{1,0:T(2,128)S(1)}, u32[]{:S(2)}, u32[]{:S(2)}) collective-permute-start(f32[2,294912]{1,0:T(2,128)S(1)} %get-tuple-element.267), channel_id=1, source_target_pairs={{8,0},{16,8},{24,16},{32,24},{40,32},{48,40},{56,48},{64,56},{72,6... | collective-permute-start | bytes 7077896 | tf_op jit(solution)/shard_map/ppermute | solution.py:29
  238.8 48.2 %collective-permute-start.3 = (f32[2,294912]{1,0:T(2,128)S(1)}, f32[2,294912]{1,0:T(2,128)S(1)}, u32[]{:S(2)}, u32[]{:S(2)}) collective-permute-start(f32[2,294912]{1,0:T(2,128)S(1)} %get-tuple-element.268), channel_id=1, source_target_pairs={{0,8},{8,16},{16,24},{24,32},{32,40},{40,48},{48,56},{56,64},{64,7... | collective-permute-start | bytes 7077896 | tf_op jit(solution)/shard_map/ppermute | solution.py:29
  289.5 1.1 copy-start.13
  302.3 308.3 %reduce-scatter.7.cloned.1.call-start = ((), (), s32[]{:S(2)}) async-start(), calls=%async_computation.4 | async-start | bytes 15040512
  328.5 1.4 copy-start.9
Sparse Core Ops, SparseCore 0:
  10.2 81.3 all-gather.1
  302.5 153.0 reduce-scatter.4
  458.0 152.5 reduce-scatter.6
where the time goes:
time: 628 us; the launch traced here: 620 us
  waiting for transfers between devices  331 us (53%)
  blocking collectives  89.1 us (14%)
  local copies, waits for them, and re-layouts  88.5 us (14%)
  matrix products  59.3 us (9%)
  other arithmetic  21.9 us (3%)
  between operations  14.5 us (2%)
  starting transfers between devices  11.2 us (2%)
    unnamed x4, waiting for transfers between devices  154 us
    psum x1, blocking collectives, body(): text_sums = lax.psum(text_total, 'slab')  89.1 us
    all_gather x1, waiting for transfers between devices, body(): full_hidden = lax.all_gather(hidden, 'head', axis=1, tiled=True)  83.6 us
    ppermute x2, waiting for transfers between devices, from_behind(): return lax.ppermute(block, axis, route)  44.5 us
    reduce_scatter x1, waiting for transfers between devices, body(): lax.psum_scatter(input_term, 'head', scatter_dimension=1, tiled=True)  34.8 us
    unnamed x32, local copies, waits for them, and re-layouts  30.2 us
    concatenate x8, local copies, waits for them, and re-layouts, own_tile(): jnp.concatenate([key_part[:nvid].reshape(nvid, width), value_part[:nvid]....  22.9 us
    ppermute x1, waiting for transfers between devices, with_halo(): after = lax.ppermute(leading, axis, down)  14.5 us
  transfers between devices with their start and end apart: 7, of which 5 were waited for; matrix products, arithmetic and copies ran while one was open for 6% of the time, Pallas kernels for 0%

commit v1 on v0

v1 whole, which is shorter than its diff:
```python
import math

import jax
import jax.numpy as jnp
from jax import lax
from jax.experimental import pallas as pl
from jax.experimental.pallas import tpu as pltpu
from jax.sharding import PartitionSpec as P

DH = 128
TILE = 384
SAMPLES = 2
HEADS_DEV = 3
CH = 384
TEXT = 256
BF = jnp.bfloat16
F32 = jnp.float32
SCALE = 1.0 / math.sqrt(DH)
EXP_SCALE = SCALE * math.log2(math.e)
MIB = 1024 * 1024

VMEM = pl.BlockSpec(memory_space=pltpu.VMEM)
SMEM = pl.BlockSpec(memory_space=pltpu.SMEM)


def dot(a, b, ca, cb):
    return lax.dot_general(a, b, (((ca,), (cb,)), ((), ())), preferred_element_type=F32)


def head_move(x, dx, dy):
    pairs = [(h, ((h // 4) ^ dx) * 4 + (h + dy) % 4) for h in range(8)]
    return lax.ppermute(x, "head", pairs)


def slab_move(x, dz, dx, dc):
    pairs = [
        (s, ((s // 4 + dz) % 4) * 4 + ((s // 2 % 2) ^ dx) * 2 + ((s % 2) ^ dc)) for s in range(16)
    ]
    return lax.ppermute(x, "slab", pairs)


def slab_step(x, distance):
    pairs = [(i, i + distance) for i in range(16) if 0 <= i + distance < 16]
    return lax.ppermute(x, "slab", pairs)


PAIRS = ((0, 0, 1), (3, 2, 4), (1, 3, 5), (2, 6, 7))


def project_kernel(meta, *refs):
    chunks, (w, q_out, kv_out, mine, other, acc) = (refs[:8], refs[8:])
    a, y, core = (meta[0], meta[1], meta[2])
    for n, (d, r0, r1) in enumerate(PAIRS):
        yj = (y + d) & 3
        pair = ((a * 4 + yj, chunks[r0]), ((1 - a) * 4 + yj, chunks[r1]))
        x = jnp.concatenate([pair[0][1][...], pair[1][1][...]], axis=1)
        for c in range(3):
            wc = jnp.concatenate([w[c, pair[0][0]], w[c, pair[1][0]]], axis=0)
            part = dot(x, wc, 1, 0)
            if n == 0:
                acc[c] = part
            else:
                acc[c] += part
        own = ((yj ^ core) & 1) == 0
        for j, ref in pair:
            z = j >> 1

            @pl.when(own)
            def _():
                mine[z] = ref[...]

            @pl.when(jnp.logical_not(own))
            def _():
                other[z] = ref[...]

    q_out[...] = acc[0].astype(BF)
    for h in range(HEADS_DEV):
        cols = slice(h * DH, (h + 1) * DH)
        kv_out[:, 2 * h * DH : (2 * h + 1) * DH] = acc[1, :, cols].astype(BF)
        kv_out[:, (2 * h + 1) * DH : (2 * h + 2) * DH] = acc[2, :, cols].astype(BF)


def project(meta, chunks, w):
    return pl.pallas_call(
        project_kernel,
        in_specs=[SMEM] + [VMEM] * 9,
        out_specs=[VMEM] * 4,
        out_shape=[
            jax.ShapeDtypeStruct((TILE, CH), BF),
            jax.ShapeDtypeStruct((TILE, 2 * CH), BF),
            jax.ShapeDtypeStruct((4, TILE, CH), BF),
            jax.ShapeDtypeStruct((4, TILE, CH), BF),
        ],
        scratch_shapes=[pltpu.VMEM((3, TILE, CH), F32)],
        compiler_params=pltpu.CompilerParams(vmem_limit_bytes=40 * MIB),
        cost_estimate=pl.CostEstimate(
            flops=2 * TILE * 3072 * 1152, bytes_accessed=14 * MIB, transcendentals=0
        ),
        name="project",
    )(meta, *chunks, w)


def attention_kernel(
    meta, adv, q_ref, prev, own, nxt, tk_ref, tv_ref, og_ref, dq, dprev, down, dnext, dtext
):
    q = q_ref[...]
    cot = (adv[0] * og_ref[...].astype(F32)).astype(BF)
    rows = lax.broadcasted_iota(jnp.int32, (TEXT, TILE), 0)
    live = rows < meta[2]
    keys = [prev[:, :DH], own[:, :DH], nxt[:, :DH], tk_ref[0]]
    vals = [prev[:, DH:], own[:, DH:], nxt[:, DH:], tv_ref[0]]
    scores = [dot(k, q, 1, 1) for k in keys]
    scores[0] = jnp.where(meta[0] > 0, scores[0], -jnp.inf)
    scores[2] = jnp.where(meta[1] > 0, scores[2], -jnp.inf)
    scores[3] = jnp.where(live, scores[3], -jnp.inf)
    top = jnp.max(scores[1], axis=0, keepdims=True)
    for n in (0, 2, 3):
        top = jnp.maximum(top, jnp.max(scores[n], axis=0, keepdims=True))
    powers = [jnp.exp2((s - top) * EXP_SCALE) for s in scores]
    total = sum(jnp.sum(p, axis=0, keepdims=True) for p in powers)
    inverse = 1.0 / total
    probs = [p * inverse for p in powers]
    probs_b = [p.astype(BF) for p in probs]
    dprobs = [dot(v, cot, 1, 1) for v in vals]
    delta = sum(
        jnp.sum(p.astype(F32) * d, axis=0, keepdims=True) for p, d in zip(probs_b, dprobs)
    )
    dscores = [(p * (d - delta) * SCALE).astype(BF) for p, d in zip(probs, dprobs)]
    grad = dot(keys[0], dscores[0], 0, 0)
    for n in (1, 2, 3):
        grad += dot(keys[n], dscores[n], 0, 0)
    dq[...] = grad.T.astype(BF)
    for n, out in ((0, dprev), (1, down), (2, dnext)):
        out[:, :DH] = dot(dscores[n], q, 1, 0).astype(out.dtype)
        out[:, DH:] = dot(probs_b[n], cot, 1, 0).astype(out.dtype)
    dtext[0] = dot(dscores[3], q, 1, 0).astype(BF)
    dtext[1] = dot(probs_b[3], cot, 1, 0).astype(BF)


def attention(sample, meta, adv, q, prev, own, nxt, text_k, text_v, out_grad):
    kv = pl.BlockSpec((TILE, 2 * DH), lambda h: (0, h))
    tile = pl.BlockSpec((TILE, DH), lambda h: (0, h))
    text = pl.BlockSpec((1, TEXT, DH), lambda h: (sample, 0, h))
    return pl.pallas_call(
        attention_kernel,
        grid=(HEADS_DEV,),
        in_specs=[
            SMEM,
            SMEM,
            tile,
            kv,
            kv,
            kv,
            text,
            text,
            pl.BlockSpec((TILE, DH), lambda h: (sample, h)),
        ],
        out_specs=[tile, kv, kv, kv, pl.BlockSpec((2, TEXT, DH), lambda h: (0, 0, h))],
        out_shape=[
            jax.ShapeDtypeStruct((TILE, CH), BF),
            jax.ShapeDtypeStruct((TILE, 2 * CH), BF),
            jax.ShapeDtypeStruct((TILE, 2 * CH), F32),
            jax.ShapeDtypeStruct((TILE, 2 * CH), BF),
            jax.ShapeDtypeStruct((2, TEXT, CH), BF),
        ],
        compiler_params=pltpu.CompilerParams(vmem_limit_bytes=40 * MIB),
        cost_estimate=pl.CostEstimate(
            flops=20 * 3 * 384 * 1408 * 128, bytes_accessed=8 * MIB, transcendentals=3 * 384 * 1408
        ),
        name="attention",
    )(meta, adv, q, prev, own, nxt, text_k, text_v, out_grad)


def hidden_kernel(meta, dq, down, low, high, w, grads, *outs):
    a, y = (meta[0], meta[1])
    kv = down[...] + low[...].astype(F32) + high[...].astype(F32)
    grads[:, :CH] = dq[...]
    for h in range(HEADS_DEV):
        cols = slice(h * DH, (h + 1) * DH)
        grads[:, CH + h * DH : CH + (h + 1) * DH] = kv[:, 2 * h * DH : (2 * h + 1) * DH].astype(BF)
        grads[:, 2 * CH + h * DH : 2 * CH + (h + 1) * DH] = kv[
            :, (2 * h + 1) * DH : (2 * h + 2) * DH
        ].astype(BF)
    for d in (2, 1, 3, 0):
        yj = (y + d) & 3
        j0, j1 = (a * 4 + yj, (1 - a) * 4 + yj)
        part = None
        for c in range(3):
            wc = jnp.concatenate([w[c, j0], w[c, j1]], axis=0)
            term = dot(grads[:, c * CH : (c + 1) * CH], wc, 1, 1)
            part = term if part is None else part + term
        outs[d][...] = part[:, :CH].astype(BF)
        outs[4 + d][...] = part[:, CH:].astype(BF)


def hidden_parts(meta, dq, down, low, high, w):
    shape = jax.ShapeDtypeStruct((TILE, CH), BF)
    return pl.pallas_call(
        hidden_kernel,
        in_specs=[SMEM] + [VMEM] * 5,
        out_specs=[VMEM] * 9,
        out_shape=[jax.ShapeDtypeStruct((TILE, 3 * CH), BF)] + [shape] * 8,
        compiler_params=pltpu.CompilerParams(vmem_limit_bytes=40 * MIB),
        cost_estimate=pl.CostEstimate(
            flops=2 * TILE * 3072 * 1152, bytes_accessed=14 * MIB, transcendentals=0
        ),
        name="hidden_parts",
    )(meta, dq, down, low, high, w)


def add(*terms):
    total = terms[0].astype(F32)
    for term in terms[1:]:
        total = total + term.astype(F32)
    return total.astype(BF)


def hidden_reduce(parts):
    same, flip = (parts[:4], parts[4:])
    far_flip = head_move(flip[2], 0, 1)
    far_same = head_move(same[2], 0, 3)
    flip_up = head_move(add(flip[1], far_flip), 0, 1)
    flip_down = head_move(flip[3], 0, 3)
    same_down = head_move(add(same[3], far_same), 0, 3)
    same_up = head_move(same[1], 0, 1)
    across = head_move(add(flip[0], flip_up, flip_down), 1, 0)
    return add(same[0], same_up, same_down, across)


def weight_kernel(meta, x0, x1, p0, p1, g0, g1, h0, h1, *outs):
    z = meta[3]
    g = jnp.concatenate([g0[...], g1[...], h0[...], h1[...]], axis=0)
    for d in (2, 1, 3, 0):
        j = (z + d) & 3
        x = jnp.concatenate([x0[j], x1[j], p0[j], p1[j]], axis=0)
        outs[d][...] = dot(x, g, 0, 0).astype(BF)


def weight_parts(meta, *arrays):
    shape = jax.ShapeDtypeStruct((CH, 3 * CH), BF)
    return pl.pallas_call(
        weight_kernel,
        in_specs=[SMEM] + [VMEM] * 8,
        out_specs=[VMEM] * 4,
        out_shape=[shape] * 4,
        compiler_params=pltpu.CompilerParams(vmem_limit_bytes=48 * MIB),
        cost_estimate=pl.CostEstimate(
            flops=2 * 768 * 3072 * 1152, bytes_accessed=16 * MIB, transcendentals=0
        ),
        name="weight_parts",
    )(meta, *arrays)


def weight_reduce(parts, x_lo, core):
    got = [slab_move(parts[d], d, 0, 0) for d in (2, 1, 3)]
    total = add(parts[0], *got)
    halves = total.reshape(2, CH // 2, 3 * CH)
    home = x_lo == core
    near = lax.dynamic_index_in_dim(halves, jnp.where(home, 1 - core, core), 0, keepdims=False)
    far = lax.dynamic_index_in_dim(halves, jnp.where(home, core, 1 - core), 0, keepdims=False)
    first, second = ([], [])
    for s in range(16):
        z, x, c = (s // 4, s // 2 % 2, s % 2)
        if x == c:
            first.append((s, z * 4 + x * 2 + 1 - c))
        else:
            first.append((s, z * 4 + (1 - x) * 2 + c))
            second.append((s, z * 4 + (1 - x) * 2 + 1 - c))
    got_first = lax.ppermute(near, "slab", first)
    got_second = lax.ppermute(far, "slab", second)
    return add(jnp.where(home, far, got_second), got_first)


def text_reduce(terms, core):
    both = jnp.stack(terms, axis=1).reshape(2, SAMPLES * TEXT, CH)
    keep = lax.dynamic_index_in_dim(both, core, 0, keepdims=False)
    give = lax.dynamic_index_in_dim(both, 1 - core, 0, keepdims=False)
    part = add(keep, slab_move(give, 0, 0, 1)).reshape(4, -1, CH)
    z = lax.axis_index("slab") // 4

    def at(d):
        return lax.dynamic_index_in_dim(part, (z + d) % 4, 0, keepdims=False)

    quarter = add(at(0), *[slab_move(at(d), d, 0, 0) for d in (2, 1, 3)])
    quarter = add(quarter, slab_move(quarter, 0, 1, 0))
    full = jnp.zeros_like(part)
    full = lax.dynamic_update_index_in_dim(full, quarter, z, 0)
    for d in (2, 1, 3):
        full = lax.dynamic_update_index_in_dim(full, slab_move(quarter, d, 0, 0), (z - d) % 4, 0)
    full = full.reshape(SAMPLES, TEXT, CH)
    twin = slab_move(full, 0, 0, 1)
    key = jnp.where(core == 0, full, twin)
    value = jnp.where(core == 0, twin, full)
    return jnp.stack([key, value], axis=2)


def gather_chunks(own):
    flip = head_move(own, 1, 0)
    below = head_move(own, 0, 1)
    above = head_move(own, 0, 3)
    flip_below = head_move(flip, 0, 1)
    flip_above = head_move(flip, 0, 3)
    far = head_move(below, 0, 1)
    far_flip = head_move(flip_above, 0, 3)
    return [own, flip, below, above, flip_below, flip_above, far, far_flip]


def body(hidden, w_qkv, text_keys, text_values, text_len, advantage, out_grad, tile_lists):
    slab = lax.axis_index("slab")
    head = lax.axis_index("head")
    core = slab % 2
    x_lo = slab // 2 % 2
    place = jnp.stack([head // 4, head % 4, core, slab // 4]).astype(jnp.int32)
    w = jnp.transpose(w_qkv, (1, 0, 2)).reshape(3, 8, CH, CH)
    index = jnp.arange(SAMPLES, dtype=jnp.int32)[:, None] + slab * SAMPLES
    has_prev = jnp.any((tile_lists == index - SAMPLES) & (tile_lists >= 0), axis=1)
    has_next = jnp.any(tile_lists == index + SAMPLES, axis=1)
    flags = jnp.stack(
        [has_prev.astype(jnp.int32), has_next.astype(jnp.int32), text_len], axis=1
    )
    dqs, grads, mines, theirs, texts, hidden_grads = ([], [], [], [], [], [])
    for s in range(SAMPLES):
        chunks = gather_chunks(hidden[s * TILE : (s + 1) * TILE])
        q, kv, mine, other = project(place, chunks, w)
        mines.append(mine)
        theirs.append(slab_move(other, 0, 0, 1))
        prev = slab_step(kv, 1)
        nxt = slab_step(kv, -1)
        dq, dprev, down, dnext, dtext = attention(
            s, flags[s], advantage[s : s + 1], q, prev, kv, nxt, text_keys, text_values, out_grad
        )
        texts.append(dtext)
        low = slab_step(dnext, 1)
        high = slab_step(dprev, -1)
        made = hidden_parts(place, dq, down, low, high, w)
        grads.append(made[0])
        hidden_grads.append(hidden_reduce(made[1:]))
    twins = [slab_move(g, 0, 0, 1) for g in grads]
    parts = weight_parts(place, *mines, *theirs, *grads, *twins)
    weight_grad = weight_reduce(parts, x_lo, core).reshape(CH // 2, 3, CH)
    text_grad = text_reduce(texts, core)
    hidden_grad = jnp.concatenate(hidden_grads, axis=0)
    return (hidden_grad, weight_grad, text_grad)


def solution(mesh):
    in_specs = (
        P("slab", "head"),
        P(None, None, "head"),
        P(None, None, "head"),
        P(None, None, "head"),
        P(),
        P(),
        P("slab", "head"),
        P("slab", None),
    )
    out_specs = (P("slab", "head"), P("slab", None, "head"), P(None, None, None, "head"))
    return jax.shard_map(body, mesh=mesh, in_specs=in_specs, out_specs=out_specs, check_vma=False)
```

time: 628 us -> 278 us (0.44)
  waiting for transfers between devices: 331 us -> 91.4 us
  blocking collectives: 89.1 us -> 0 us
  starting transfers between devices: 11.2 us -> 95.7 us
  local copies, waits for them, and re-layouts: 88.5 us -> 28.5 us
  matrix products: 59.3 us -> 0 us
  Pallas kernels: 0 us -> 48 us
  other arithmetic: 21.9 us -> 8.47 us
  between operations: 14.5 us -> 1.5 us
    unnamed x4 -> x0, waiting for transfers between devices: 154 us -> none
    psum x1 -> x0, blocking collectives: 89.1 us -> none  [body(): text_sums = lax.psum(text_total, 'slab')]
    ppermute x4 -> x54, starting transfers between devices: 11.1 us -> 95.7 us  [the longest x16 32.4 us: slab_move(): return lax.ppermute(x, 'slab', pairs)]
    all_gather x1 -> x0, waiting for transfers between devices: 83.6 us -> none  [body(): full_hidden = lax.all_gather(hidden, 'head', axis=1, tiled=True)]
    dot_general x16 -> x0, matrix products: 59.3 us -> none  [the longest x1 11.7 us: body(): jnp.einsum('tch,dch->td', grads, w_qkv, preferred_element_type=jnp.float32)]
    pallas_call x0 -> x7, Pallas kernels: none -> 48 us  [the longest x2 18.1 us: attention(): pl.pallas_call(attention_kernel, grid=(HEADS_DEV,), in_specs=[SMEM, SMEM,...]
    reduce_scatter x1 -> x0, waiting for transfers between devices: 34.8 us -> none  [body(): lax.psum_scatter(input_term, 'head', scatter_dimension=1, tiled=True)]
    ppermute x4 -> x54, waiting for transfers between devices: 59.1 us -> 91.4 us  [the longest x16 41.6 us: slab_move(): return lax.ppermute(x, 'slab', pairs)]
  transfers between devices with their start and end apart: 7 -> 54, of which waited for: 5 -> 18; matrix products, arithmetic and copies ran while one was open for 6% -> 4% of each run, Pallas kernels for 0% -> 14%
where the time goes in v1:
time: 278 us; the launch traced here: 273 us
  starting transfers between devices  95.7 us (34%)
  waiting for transfers between devices  91.4 us (33%)
  Pallas kernels  48 us (17%)
  local copies, waits for them, and re-layouts  28.5 us (10%)
  other arithmetic  8.47 us (3%)
    ppermute x16, waiting for transfers between devices, slab_move(): return lax.ppermute(x, 'slab', pairs)  41.6 us
    ppermute x28, waiting for transfers between devices, head_move(): return lax.ppermute(x, 'head', pairs)  37.3 us
    ppermute x16, starting transfers between devices, slab_move(): return lax.ppermute(x, 'slab', pairs)  32.4 us
    ppermute x28, starting transfers between devices, head_move(): return lax.ppermute(x, 'head', pairs)  31.3 us
    ppermute x8, starting transfers between devices, slab_step(): return lax.ppermute(x, 'slab', pairs)  23.8 us
    unnamed x61, local copies, waits for them, and re-layouts  21.4 us
    pallas_call x2, Pallas kernels, attention(): pl.pallas_call(attention_kernel, grid=(HEADS_DEV,), in_specs=[SMEM, SMEM,...  18.1 us
    pallas_call x2, Pallas kernels, hidden_parts(): pl.pallas_call(hidden_kernel, in_specs=[SMEM] + [VMEM] * 5, out_specs=[VM...  10.5 us
  transfers between devices with their start and end apart: 54, of which 18 were waited for; matrix products, arithmetic and copies ran while one was open for 4% of the time, Pallas kernels for 14%

profile of v1, /device:TPU:1, one launch (start us, length us, event | category | flops | bytes accessed | tf_op | source)
XLA Modules:
  0.0 273.5 jit_solution(11901809628458987074)
XLA Ops:
  0.6 1.1 fusion.6
  1.8 3.7 %collective-permute-start.18 = (bf16[384,384]{1,0:T(8,128)(2,1)S(1)}, bf16[384,384]{1,0:T(8,128)(2,1)S(1)}, u32[]{:S(2)}, u32[]{:S(2)}) collective-permute-start(bf16[384,384]{1,0:T(8,128)(2,1)S(1)} %get-tuple-element.97.refs_0_), channel_id=1, source_target_pairs={{0,4},{1,5},{2,6},{3,7},{4,0},{5,1},{6,2},{7,3},{8,12},{9,13},{10,... | collective-permute-start | bytes 884744 | tf_op jit(solution)/shard_map/ppermute | solution.py:32
  5.4 1.3 collective-permute-start.19
  6.7 1.4 collective-permute-start.20
  8.4 3.3 %collective-permute-done.18.refs_1_ = bf16[384,384]{1,0:T(8,128)(2,1)S(1)} collective-permute-done((bf16[384,384]{1,0:T(8,128)(2,1)S(1)}, bf16[384,384]{1,0:T(8,128)(2,1)S(1)}, u32[]{:S(2)}, u32[]{:S(2)}) %collective-permute-start.18) | collective-permute-done | bytes 294944 | tf_op jit(solution)/shard_map/ppermute | solution.py:32
  11.7 3.1 %collective-permute-start.22 = (bf16[384,384]{1,0:T(8,128)(2,1)S(1)}, bf16[384,384]{1,0:T(8,128)(2,1)S(1)}, u32[]{:S(2)}, u32[]{:S(2)}) collective-permute-start(bf16[384,384]{1,0:T(8,128)(2,1)S(1)} %collective-permute-done.18.refs_1_), channel_id=1, source_target_pairs={{0,3},{1,0},{2,1},{3,2},{4,7},{5,4},{6,5},{7,6},{8,11},{9,8},{10,9... | collective-permute-start | bytes 884744 | tf_op jit(solution)/shard_map/ppermute | solution.py:32
  15.6 2.4 collective-permute-done.refs_1_
  17.9 3.2 %collective-permute-start.4 = (bf16[384,384]{1,0:T(8,128)(2,1)S(1)}, bf16[384,384]{1,0:T(8,128)(2,1)}, u32[]{:S(2)}, u32[]{:S(2)}) collective-permute-start(bf16[384,384]{1,0:T(8,128)(2,1)S(1)} %collective-permute-done.refs_1_), channel_id=1, source_target_pairs={{0,3},{1,0},{2,1},{3,2},{4,7},{5,4},{6,5},{7,6},{8,11},{9,8},{10,9... | collective-permute-start | bytes 884744 | tf_op jit(solution)/shard_map/ppermute | solution.py:32
  22.5 4.4 %collective-permute-done.21.refs_4_ = bf16[384,384]{1,0:T(8,128)(2,1)S(1)} collective-permute-done((bf16[384,384]{1,0:T(8,128)(2,1)S(1)}, bf16[384,384]{1,0:T(8,128)(2,1)S(1)}, u32[]{:S(2)}, u32[]{:S(2)}) %collective-permute-start.21) | collective-permute-done | bytes 294944 | tf_op jit(solution)/shard_map/ppermute | solution.py:32
  27.7 5.5 %collective-permute-done.23.refs_6_ = bf16[384,384]{1,0:T(8,128)(2,1)S(1)} collective-permute-done((bf16[384,384]{1,0:T(8,128)(2,1)S(1)}, bf16[384,384]{1,0:T(8,128)(2,1)S(1)}, u32[]{:S(2)}, u32[]{:S(2)}) %collective-permute-start.23) | collective-permute-done | bytes 294944 | tf_op jit(solution)/shard_map/ppermute | solution.py:32
  34.0 2.7 collective-permute-start.6
  37.4 3.0 %copy-done = bf16[3072,3,384]{2,0,1:T(8,128)(2,1)S(1)} copy-done((bf16[3072,3,384]{2,0,1:T(8,128)(2,1)S(1)}, bf16[3072,3,384]{2,0,1:T(8,128)(2,1)}, u32[]{:S(2)}) %copy-start) | copy-done | bytes 7077912
  43.3 4.9 %project.3 = (bf16[384,384]{1,0:T(8,128)(2,1)S(1)}, bf16[384,768]{1,0:T(8,128)(2,1)S(1)}, bf16[4,384,384]{2,1,0:T(8,128)(2,1)S(1)}, bf16[4,384,384]{2,1,0:T(8,128)(2,1)S(1)}) custom-call(s32[4]{0:T(128)S(1)} %pad_add_fusion.1.meta, bf16[384,384]{1,0:T(8,128)(2,1)S(1)} %get-tuple-element.97.refs_0_, bf16[384,384]{1,0:T(8,128)(2,1)S(1)} %collective-permute-done.18.refs_1_, ...), custom_call_target="tpu_custom_call" | custom-call | flops 2717908992 | bytes 14680064 | tf_op jit(solution)/shard_map/project/pallas_call | solution.py:84
  49.2 5.9 %collective-permute-start.25 = (bf16[384,768]{1,0:T(8,128)(2,1)S(1)}, bf16[384,768]{1,0:T(8,128)(2,1)S(1)}, u32[]{:S(2)}, u32[]{:S(2)}) collective-permute-start(bf16[384,768]{1,0:T(8,128)(2,1)S(1)} %get-tuple-element.58.own), channel_id=1, source_target_pairs={{0,8},{8,16},{16,24},{24,32},{32,40},{40,48},{48,56},{56,64},{64,7... | collective-permute-start | bytes 1769480 | tf_op jit(solution)/shard_map/ppermute | solution.py:44
  55.1 1.9 collective-permute-start.26
  57.7 5.5 %project.2 = (bf16[384,384]{1,0:T(8,128)(2,1)S(1)}, bf16[384,768]{1,0:T(8,128)(2,1)S(1)}, bf16[4,384,384]{2,1,0:T(8,128)(2,1)S(1)}, bf16[4,384,384]{2,1,0:T(8,128)(2,1)S(1)}) custom-call(s32[4]{0:T(128)S(1)} %pad_add_fusion.1.meta, bf16[384,384]{1,0:T(8,128)(2,1)S(1)} %get-tuple-element.96.refs_0_, bf16[384,384]{1,0:T(8,128)(2,1)S(1)} %collective-permute-done.refs_1_, ...), custom_call_target="tpu_custom_call" | custom-call | flops 2717908992 | bytes 14680064 | tf_op jit(solution)/shard_map/project/pallas_call | solution.py:84
  64.2 3.9 %collective-permute-start.7 = (bf16[384,768]{1,0:T(8,128)(2,1)S(1)}, bf16[384,768]{1,0:T(8,128)(2,1)S(1)}, u32[]{:S(2)}, u32[]{:S(2)}) collective-permute-start(bf16[384,768]{1,0:T(8,128)(2,1)S(1)} %get-tuple-element.44.own), channel_id=1, source_target_pairs={{0,8},{8,16},{16,24},{24,32},{32,40},{40,48},{48,56},{56,64},{64,7... | collective-permute-start | bytes 1769480 | tf_op jit(solution)/shard_map/ppermute | solution.py:44
  68.1 1.9 collective-permute-start.8
  71.2 9.4 %attention.3 = (bf16[384,384]{1,0:T(8,128)(2,1)S(1)}, bf16[384,768]{1,0:T(8,128)(2,1)}, f32[384,768]{1,0:T(8,128)S(1)}, bf16[384,768]{1,0:T(8,128)(2,1)}, bf16[2,256,384]{2,1,0:T(8,128)(2,1)S(1)}) custom-call(s32[3]{0:T(128)S(1)} %get-tuple-element.87.meta, f32[1]{0:T(128)} %get-tuple-element.102.adv, bf16[384,384]{1,0:T(8,128)(2,1)S(1)} %get-tuple-element.57.q_ref, ...), custom_call_target="tpu_custom_call" | custom-call | flops 4152360960 | bytes 8388608 | tf_op jit(solution)/shard_map/attention/pallas_call | solution.py:144
  81.3 3.5 %collective-permute-done.8.nxt = bf16[384,768]{1,0:T(8,128)(2,1)S(1)} collective-permute-done((bf16[384,768]{1,0:T(8,128)(2,1)S(1)}, bf16[384,768]{1,0:T(8,128)(2,1)S(1)}, u32[]{:S(2)}, u32[]{:S(2)}) %collective-permute-start.8) | collective-permute-done | bytes 589856 | tf_op jit(solution)/shard_map/ppermute | solution.py:44
  84.8 8.7 %attention.2 = (bf16[384,384]{1,0:T(8,128)(2,1)S(1)}, bf16[384,768]{1,0:T(8,128)(2,1)S(1)}, f32[384,768]{1,0:T(8,128)S(1)}, bf16[384,768]{1,0:T(8,128)(2,1)S(1)}, bf16[2,256,384]{2,1,0:T(8,128)(2,1)S(1)}) custom-call(s32[3]{0:T(128)S(1)} %get-tuple-element.86.meta, f32[1]{0:T(128)} %get-tuple-element.101.adv, bf16[384,384]{1,0:T(8,128)(2,1)S(1)} %get-tuple-element.43.q_ref, ...), custom_call_target="tpu_custom_call" | custom-call | flops 4152360960 | bytes 8388608 | tf_op jit(solution)/shard_map/attention/pallas_call | solution.py:144
  96.4 2.1 collective-permute-done.45
  98.5 1.2 fusion
  101.1 2.6 collective-permute-start.48
  103.7 2.2 collective-permute-start.46
  105.9 2.6 collective-permute-start.27
  108.5 2.5 collective-permute-start.28
  111.0 3.0 %collective-permute-start.9 = (bf16[384,768]{1,0:T(8,128)(2,1)S(1)}, bf16[384,768]{1,0:T(8,128)(2,1)}, u32[]{:S(2)}, u32[]{:S(2)}) collective-permute-start(bf16[384,768]{1,0:T(8,128)(2,1)S(1)} %get-tuple-element.47), channel_id=1, source_target_pairs={{0,8},{8,16},{16,24},{24,32},{32,40},{40,48},{48,56},{56,64},{64,7... | collective-permute-start | bytes 1769480 | tf_op jit(solution)/shard_map/ppermute | solution.py:44
  114.1 2.1 collective-permute-start.10
  116.2 1.7 fusion.3
  118.0 3.4 %collective-permute-start.49 = (bf16[128,384]{1,0:T(8,128)(2,1)}, bf16[128,384]{1,0:T(8,128)(2,1)}, u32[]{:S(2)}, u32[]{:S(2)}) collective-permute-start(bf16[128,384]{1,0:T(8,128)(2,1)} %fusion.3), channel_id=1, source_target_pairs={{0,16},{8,24},{16,0},{24,8},{32,48},{40,56},{48,32},{56,40},{64,80... | collective-permute-start | bytes 294920 | tf_op jit(solution)/shard_map/ppermute | solution.py:39
  121.3 17.1 %collective-permute-done.49 = bf16[128,384]{1,0:T(8,128)(2,1)} collective-permute-done((bf16[128,384]{1,0:T(8,128)(2,1)}, bf16[128,384]{1,0:T(8,128)(2,1)}, u32[]{:S(2)}, u32[]{:S(2)}) %collective-permute-start.49) | collective-permute-done | bytes 98336 | tf_op jit(solution)/shard_map/ppermute | solution.py:39
  138.4 2.1 collective-permute-start.36
  141.2 1.6 bitcast_dynamic-update-slice_fusion.3
  143.6 3.0 %copy-done.2 = bf16[3072,3,384]{2,0,1:T(8,128)(2,1)S(1)} copy-done((bf16[3072,3,384]{2,0,1:T(8,128)(2,1)S(1)}, bf16[3072,3,384]{2,0,1:T(8,128)(2,1)}, u32[]{:S(2)}) %copy-start.2) | copy-done | bytes 7077912
  146.6 1.3 copy-done.15
  148.8 5.3 %hidden_parts.3 = (bf16[384,1152]{1,0:T(8,128)(2,1)S(1)}, bf16[384,384]{1,0:T(8,128)(2,1)S(1)}, bf16[384,384]{1,0:T(8,128)(2,1)S(1)}, bf16[384,384]{1,0:T(8,128)...) custom-call(s32[4]{0:T(128)S(1)} %pad_add_fusion.1.meta, ...), custom_call_target="tpu_custom_call" | custom-call | flops 2717908992 | bytes 14680064 | tf_op jit(solution)/shard_map/hidden_parts/pallas_call | solution.py:198
  154.1 8.9 %collective-permute-start.51 = (bf16[128,384]{1,0:T(8,128)(2,1)S(1)}, bf16[128,384]{1,0:T(8,128)(2,1)S(1)}, u32[]{:S(2)}, u32[]{:S(2)}) collective-permute-start(bf16[128,384]{1,0:T(8,128)(2,1)S(1)} %get-tuple-element.91), channel_id=1, source_target_pairs={{0,32},{8,40},{16,48},{24,56},{32,64},{40,72},{48,80},{56,88},{64,... | collective-permute-start | bytes 294920 | tf_op jit(solution)/shard_map/ppermute | solution.py:39
  163.0 2.7 collective-permute-start.52
  165.7 5.2 %hidden_parts.2 = (bf16[384,1152]{1,0:T(8,128)(2,1)S(1)}, bf16[384,384]{1,0:T(8,128)(2,1)S(1)}, bf16[384,384]{1,0:T(8,128)(2,1)S(1)}, bf16[384,384]{1,0:T(8,128)...) custom-call(s32[4]{0:T(128)S(1)} %pad_add_fusion.1.meta, ...), custom_call_target="tpu_custom_call" | custom-call | flops 2717908992 | bytes 14680064 | tf_op jit(solution)/shard_map/hidden_parts/pallas_call | solution.py:198
  171.6 2.7 collective-permute-start.30
  175.6 3.8 %collective-permute-done.32 = bf16[384,384]{1,0:T(8,128)(2,1)S(1)} collective-permute-done((bf16[384,384]{1,0:T(8,128)(2,1)S(1)}, bf16[384,384]{1,0:T(8,128)(2,1)S(1)}, u32[]{:S(2)}, u32[]{:S(2)}) %collective-permute-start.32) | collective-permute-done | bytes 294944 | tf_op jit(solution)/shard_map/ppermute | solution.py:32
  179.4 4.0 %collective-permute-start.38 = (bf16[384,1152]{1,0:T(8,128)(2,1)S(1)}, bf16[384,1152]{1,0:T(8,128)(2,1)S(1)}, u32[]{:S(2)}, u32[]{:S(2)}) collective-permute-start(bf16[384,1152]{1,0:T(8,128)(2,1)S(1)} %get-tuple-element.75.g0), channel_id=1, source_target_pairs={{0,8},{8,0},{16,24},{24,16},{32,40},{40,32},{48,56},{56,48},{64,72... | collective-permute-start | bytes 2654216 | tf_op jit(solution)/shard_map/ppermute | solution.py:39
  183.5 2.3 collective-permute-done.14
  185.9 6.1 %collective-permute-done.12 = bf16[384,384]{1,0:T(8,128)(2,1)S(1)} collective-permute-done((bf16[384,384]{1,0:T(8,128)(2,1)S(1)}, bf16[384,384]{1,0:T(8,128)(2,1)S(1)}, u32[]{:S(2)}, u32[]{:S(2)}) %collective-permute-start.12) | collective-permute-done | bytes 294944 | tf_op jit(solution)/shard_map/ppermute | solution.py:32
  192.0 1.5 collective-permute-start.34
  193.6 3.2 %collective-permute-start.53 = (bf16[2,256,384]{2,1,0:T(8,128)(2,1)}, bf16[2,256,384]{2,1,0:T(8,128)(2,1)S(1)}, u32[]{:S(2)}, u32[]{:S(2)}) collective-permute-start(bf16[2,256,384]{2,1,0:T(8,128)(2,1)} %bitcast.27), channel_id=1, source_target_pairs={{0,8},{8,0},{16,24},{24,16},{32,40},{40,32},{48,56},{56,48},{64,72... | collective-permute-start | bytes 1179656 | tf_op jit(solution)/shard_map/ppermute | solution.py:39
  198.2 8.9 %weight_parts.1 = (bf16[384,1152]{1,0:T(8,128)(2,1)S(1)}, bf16[384,1152]{1,0:T(8,128)(2,1)S(1)}, bf16[384,1152]{1,0:T(8,128)(2,1)S(1)}, bf16[384,1152]{1,0:T(8,128)(2,1)S(1)}) custom-call(s32[4]{0:T(128)S(1)} %pad_add_fusion.1.meta, bf16[4,384,384]{2,1,0:T(8,128)(2,1)} %copy-done.17, bf16[4,384,384]{2,1,0:T(8,128)(2,1)} %copy-done.16, ...), custom_call_target="tpu_custom_call" | custom-call | flops 5435817984 | bytes 16777216 | tf_op jit(solution)/shard_map/weight_parts/pallas_call | solution.py:241
  207.5 1.2 collective-permute-start.41
  208.6 1.3 collective-permute-start.40
  211.1 2.3 collective-permute-start.16
  213.5 1.7 copy.14
  215.3 3.2 %collective-permute-done.16 = bf16[384,384]{1,0:T(8,128)(2,1)S(1)} collective-permute-done((bf16[384,384]{1,0:T(8,128)(2,1)S(1)}, bf16[384,384]{1,0:T(8,128)(2,1)S(1)}, u32[]{:S(2)}, u32[]{:S(2)}) %collective-permute-start.16) | collective-permute-done | bytes 294944 | tf_op jit(solution)/shard_map/ppermute | solution.py:32
  218.8 2.8 %collective-permute-done.15 = bf16[384,384]{1,0:T(8,128)(2,1)S(1)} collective-permute-done((bf16[384,384]{1,0:T(8,128)(2,1)S(1)}, bf16[384,384]{1,0:T(8,128)(2,1)S(1)}, u32[]{:S(2)}, u32[]{:S(2)}) %collective-permute-start.15) | collective-permute-done | bytes 294944 | tf_op jit(solution)/shard_map/ppermute | solution.py:32
  221.7 6.4 %collective-permute-done.42 = bf16[384,1152]{1,0:T(8,128)(2,1)S(1)} collective-permute-done((bf16[384,1152]{1,0:T(8,128)(2,1)S(1)}, bf16[384,1152]{1,0:T(8,128)(2,1)S(1)}, u32[]{:S(2)}, u32[]{:S(2)}) %collective-permute-start.42) | collective-permute-done | bytes 884768 | tf_op jit(solution)/shard_map/ppermute | solution.py:39
  228.2 2.1 collective-permute-start.31
  230.3 1.6 collective-permute-start.13
  231.9 16.1 %collective-permute-done.40 = bf16[384,1152]{1,0:T(8,128)(2,1)S(1)} collective-permute-done((bf16[384,1152]{1,0:T(8,128)(2,1)S(1)}, bf16[384,1152]{1,0:T(8,128)(2,1)S(1)}, u32[]{:S(2)}, u32[]{:S(2)}) %collective-permute-start.40) | collective-permute-done | bytes 884768 | tf_op jit(solution)/shard_map/ppermute | solution.py:39
  248.0 1.7 collective-permute-start.35
  250.1 1.4 collective-permute-start.17
  251.6 3.4 %collective-permute-done.35 = bf16[384,384]{1,0:T(8,128)(2,1)S(1)} collective-permute-done((bf16[384,384]{1,0:T(8,128)(2,1)S(1)}, bf16[384,384]{1,0:T(8,128)(2,1)S(1)}, u32[]{:S(2)}, u32[]{:S(2)}) %collective-permute-start.35) | collective-permute-done | bytes 294944 | tf_op jit(solution)/shard_map/ppermute | solution.py:32
  255.0 8.1 %collective-permute-start.43 = (bf16[192,1152]{1,0:T(8,128)(2,1)S(1)}, bf16[192,1152]{1,0:T(8,128)(2,1)S(1)}, u32[]{:S(2)}, u32[]{:S(2)}) collective-permute-start(bf16[192,1152]{1,0:T(8,128)(2,1)S(1)} %get-tuple-element.92), channel_id=1, source_target_pairs={{8,16},{16,8},{40,48},{48,40},{72,80},{80,72},{104,112},{112,104},... | collective-permute-start | bytes 1327112 | tf_op jit(solution)/shard_map/ppermute | solution.py:270
  264.3 3.0 %collective-permute-done.44 = bf16[192,1152]{1,0:T(8,128)(2,1)S(1)} collective-permute-done((bf16[192,1152]{1,0:T(8,128)(2,1)S(1)}, bf16[192,1152]{1,0:T(8,128)(2,1)S(1)}, u32[]{:S(2)}, u32[]{:S(2)}) %collective-permute-start.44) | collective-permute-done | bytes 442400 | tf_op jit(solution)/shard_map/ppermute | solution.py:269
  267.3 5.0 %collective-permute-done.43 = bf16[192,1152]{1,0:T(8,128)(2,1)S(1)} collective-permute-done((bf16[192,1152]{1,0:T(8,128)(2,1)S(1)}, bf16[192,1152]{1,0:T(8,128)(2,1)S(1)}, u32[]{:S(2)}, u32[]{:S(2)}) %collective-permute-start.43) | collective-permute-done | bytes 442400 | tf_op jit(solution)/shard_map/ppermute | solution.py:270
  (147 shorter events, 27.2 us)
Async XLA Ops:
  0.6 14.2 %copy-start.25 = (s32[2,3]{1,0:T(2,128)S(1)}, s32[2,3]{1,0:T(2,128)}, u32[]{:S(2)}) copy-start(s32[2,3]{1,0:T(2,128)} %param.15) | copy-start | bytes 76
  1.8 9.9 %collective-permute-start.18 = (bf16[384,384]{1,0:T(8,128)(2,1)S(1)}, bf16[384,384]{1,0:T(8,128)(2,1)S(1)}, u32[]{:S(2)}, u32[]{:S(2)}) collective-permute-start(bf16[384,384]{1,0:T(8,128)(2,1)S(1)} %get-tuple-element.97.refs_0_), channel_id=1, source_target_pairs={{0,4},{1,5},{2,6},{3,7},{4,0},{5,1},{6,2},{7,3},{8,12},{9,13},{10,... | collective-permute-start | bytes 884744 | tf_op jit(solution)/shard_map/ppermute | solution.py:32
  5.4 9.6 %collective-permute-start.19 = (bf16[384,384]{1,0:T(8,128)(2,1)S(1)}, bf16[384,384]{1,0:T(8,128)(2,1)S(1)}, u32[]{:S(2)}, u32[]{:S(2)}) collective-permute-start(bf16[384,384]{1,0:T(8,128)(2,1)S(1)} %get-tuple-element.97.refs_0_), channel_id=1, source_target_pairs={{0,1},{1,2},{2,3},{3,0},{4,5},{5,6},{6,7},{7,4},{8,9},{9,10},{10,1... | collective-permute-start | bytes 884744 | tf_op jit(solution)/shard_map/ppermute | solution.py:32
  6.7 8.4 %collective-permute-start.20 = (bf16[384,384]{1,0:T(8,128)(2,1)S(1)}, bf16[384,384]{1,0:T(8,128)(2,1)S(1)}, u32[]{:S(2)}, u32[]{:S(2)}) collective-permute-start(bf16[384,384]{1,0:T(8,128)(2,1)S(1)} %get-tuple-element.97.refs_0_), channel_id=1, source_target_pairs={{0,3},{1,0},{2,1},{3,2},{4,7},{5,4},{6,5},{7,6},{8,11},{9,8},{10,9... | collective-permute-start | bytes 884744 | tf_op jit(solution)/shard_map/ppermute | solution.py:32
  8.2 9.8 %collective-permute-start = (bf16[384,384]{1,0:T(8,128)(2,1)S(1)}, bf16[384,384]{1,0:T(8,128)(2,1)S(1)}, u32[]{:S(2)}, u32[]{:S(2)}) collective-permute-start(bf16[384,384]{1,0:T(8,128)(2,1)S(1)} %get-tuple-element.96.refs_0_), channel_id=1, source_target_pairs={{0,4},{1,5},{2,6},{3,7},{4,0},{5,1},{6,2},{7,3},{8,12},{9,13},{10,... | collective-permute-start | bytes 884744 | tf_op jit(solution)/shard_map/ppermute | solution.py:32
  8.4 13.5 %collective-permute-start.1 = (bf16[384,384]{1,0:T(8,128)(2,1)S(1)}, bf16[384,384]{1,0:T(8,128)(2,1)S(1)}, u32[]{:S(2)}, u32[]{:S(2)}) collective-permute-start(bf16[384,384]{1,0:T(8,128)(2,1)S(1)} %get-tuple-element.96.refs_0_), channel_id=1, source_target_pairs={{0,1},{1,2},{2,3},{3,0},{4,5},{5,6},{6,7},{7,4},{8,9},{9,10},{10,1... | collective-permute-start | bytes 884744 | tf_op jit(solution)/shard_map/ppermute | solution.py:32
  11.7 9.4 %collective-permute-start.22 = (bf16[384,384]{1,0:T(8,128)(2,1)S(1)}, bf16[384,384]{1,0:T(8,128)(2,1)S(1)}, u32[]{:S(2)}, u32[]{:S(2)}) collective-permute-start(bf16[384,384]{1,0:T(8,128)(2,1)S(1)} %collective-permute-done.18.refs_1_), channel_id=1, source_target_pairs={{0,3},{1,0},{2,1},{3,2},{4,7},{5,4},{6,5},{7,6},{8,11},{9,8},{10,9... | collective-permute-start | bytes 884744 | tf_op jit(solution)/shard_map/ppermute | solution.py:32
  15.1 11.9 %collective-permute-start.21 = (bf16[384,384]{1,0:T(8,128)(2,1)S(1)}, bf16[384,384]{1,0:T(8,128)(2,1)S(1)}, u32[]{:S(2)}, u32[]{:S(2)}) collective-permute-start(bf16[384,384]{1,0:T(8,128)(2,1)S(1)} %collective-permute-done.18.refs_1_), channel_id=1, source_target_pairs={{0,1},{1,2},{2,3},{3,0},{4,5},{5,6},{6,7},{7,4},{8,9},{9,10},{10,1... | collective-permute-start | bytes 884744 | tf_op jit(solution)/shard_map/ppermute | solution.py:32
  15.2 18.1 %collective-permute-start.23 = (bf16[384,384]{1,0:T(8,128)(2,1)S(1)}, bf16[384,384]{1,0:T(8,128)(2,1)S(1)}, u32[]{:S(2)}, u32[]{:S(2)}) collective-permute-start(bf16[384,384]{1,0:T(8,128)(2,1)S(1)} %collective-permute-done.19.refs_2_), channel_id=1, source_target_pairs={{0,1},{1,2},{2,3},{3,0},{4,5},{5,6},{6,7},{7,4},{8,9},{9,10},{10,1... | collective-permute-start | bytes 884744 | tf_op jit(solution)/shard_map/ppermute | solution.py:32
  17.9 16.1 %collective-permute-start.4 = (bf16[384,384]{1,0:T(8,128)(2,1)S(1)}, bf16[384,384]{1,0:T(8,128)(2,1)}, u32[]{:S(2)}, u32[]{:S(2)}) collective-permute-start(bf16[384,384]{1,0:T(8,128)(2,1)S(1)} %collective-permute-done.refs_1_), channel_id=1, source_target_pairs={{0,3},{1,0},{2,1},{3,2},{4,7},{5,4},{6,5},{7,6},{8,11},{9,8},{10,9... | collective-permute-start | bytes 884744 | tf_op jit(solution)/shard_map/ppermute | solution.py:32
  21.1 15.6 %collective-permute-start.24 = (bf16[384,384]{1,0:T(8,128)(2,1)S(1)}, bf16[384,384]{1,0:T(8,128)(2,1)S(1)}, u32[]{:S(2)}, u32[]{:S(2)}) collective-permute-start(bf16[384,384]{1,0:T(8,128)(2,1)S(1)} %collective-permute-done.22.refs_5_), channel_id=1, source_target_pairs={{0,3},{1,0},{2,1},{3,2},{4,7},{5,4},{6,5},{7,6},{8,11},{9,8},{10,9... | collective-permute-start | bytes 884744 | tf_op jit(solution)/shard_map/ppermute | solution.py:32
  21.9 33.2 %collective-permute-start.2 = (bf16[384,384]{1,0:T(8,128)(2,1)S(1)}, bf16[384,384]{1,0:T(8,128)(2,1)}, u32[]{:S(2)}, u32[]{:S(2)}) collective-permute-start(bf16[384,384]{1,0:T(8,128)(2,1)S(1)} %get-tuple-element.96.refs_0_), channel_id=1, source_target_pairs={{0,3},{1,0},{2,1},{3,2},{4,7},{5,4},{6,5},{7,6},{8,11},{9,8},{10,9... | collective-permute-start | bytes 884744 | tf_op jit(solution)/shard_map/ppermute | solution.py:32
  27.7 30.0 %collective-permute-start.3 = (bf16[384,384]{1,0:T(8,128)(2,1)S(1)}, bf16[384,384]{1,0:T(8,128)(2,1)S(1)}, u32[]{:S(2)}, u32[]{:S(2)}) collective-permute-start(bf16[384,384]{1,0:T(8,128)(2,1)S(1)} %collective-permute-done.refs_1_), channel_id=1, source_target_pairs={{0,1},{1,2},{2,3},{3,0},{4,5},{5,6},{6,7},{7,4},{8,9},{9,10},{10,1... | collective-permute-start | bytes 884744 | tf_op jit(solution)/shard_map/ppermute | solution.py:32
  34.0 23.6 %collective-permute-start.5 = (bf16[384,384]{1,0:T(8,128)(2,1)S(1)}, bf16[384,384]{1,0:T(8,128)(2,1)S(1)}, u32[]{:S(2)}, u32[]{:S(2)}) collective-permute-start(bf16[384,384]{1,0:T(8,128)(2,1)S(1)} %collective-permute-done.1.refs_2_), channel_id=1, source_target_pairs={{0,1},{1,2},{2,3},{3,0},{4,5},{5,6},{6,7},{7,4},{8,9},{9,10},{10,1... | collective-permute-start | bytes 884744 | tf_op jit(solution)/shard_map/ppermute | solution.py:32
  34.0 23.7 %collective-permute-start.6 = (bf16[384,384]{1,0:T(8,128)(2,1)}, bf16[384,384]{1,0:T(8,128)(2,1)S(1)}, u32[]{:S(2)}, u32[]{:S(2)}) collective-permute-start(bf16[384,384]{1,0:T(8,128)(2,1)} %collective-permute-done.4.refs_5_), channel_id=1, source_target_pairs={{0,3},{1,0},{2,1},{3,2},{4,7},{5,4},{6,5},{7,6},{8,11},{9,8},{10,9... | collective-permute-start | bytes 884744 | tf_op jit(solution)/shard_map/ppermute | solution.py:32
  43.3 13.7 %copy-start.24 = (f32[2]{0:T(128)S(1)}, f32[2]{0:T(128)}, u32[]{:S(2)}) copy-start(f32[2]{0:T(128)} %param.13) | copy-start | bytes 28
  43.3 14.4 %copy-start.1 = (bf16[3072,3,384]{2,0,1:T(8,128)(2,1)S(1)}, bf16[3072,3,384]{2,0,1:T(8,128)(2,1)}, u32[]{:S(2)}) copy-start(bf16[3072,3,384]{2,0,1:T(8,128)(2,1)} %param.9) | copy-start | bytes 21233668
  49.2 21.0 %collective-permute-start.25 = (bf16[384,768]{1,0:T(8,128)(2,1)S(1)}, bf16[384,768]{1,0:T(8,128)(2,1)S(1)}, u32[]{:S(2)}, u32[]{:S(2)}) collective-permute-start(bf16[384,768]{1,0:T(8,128)(2,1)S(1)} %get-tuple-element.58.own), channel_id=1, source_target_pairs={{0,8},{8,16},{16,24},{24,32},{32,40},{40,48},{48,56},{56,64},{64,7... | collective-permute-start | bytes 1769480 | tf_op jit(solution)/shard_map/ppermute | solution.py:44
  55.1 16.1 %collective-permute-start.26 = (bf16[384,768]{1,0:T(8,128)(2,1)S(1)}, bf16[384,768]{1,0:T(8,128)(2,1)S(1)}, u32[]{:S(2)}, u32[]{:S(2)}) collective-permute-start(bf16[384,768]{1,0:T(8,128)(2,1)S(1)} %get-tuple-element.58.own), channel_id=1, source_target_pairs={{8,0},{16,8},{24,16},{32,24},{40,32},{48,40},{56,48},{64,56},{72,6... | collective-permute-start | bytes 1769480 | tf_op jit(solution)/shard_map/ppermute | solution.py:44
  57.6 12.4 %copy-start.26 = (s32[2]{0:T(128)S(1)}, s32[2]{0:T(128)}, u32[]{:S(2)}) copy-start(s32[2]{0:T(128)} %param.12) | copy-start | bytes 28
  57.6 13.5 %copy-start.3 = (bf16[768,384]{1,0:T(8,128)(2,1)S(1)}, bf16[768,384]{1,0:T(8,128)(2,1)}, u32[]{:S(2)}) copy-start(bf16[768,384]{1,0:T(8,128)(2,1)} %og_ref.3) | copy-start | bytes 1769476
  57.6 13.5 %copy-start.4 = (bf16[2,256,384]{2,1,0:T(8,128)(2,1)S(1)}, bf16[2,256,384]{2,1,0:T(8,128)(2,1)}, u32[]{:S(2)}) copy-start(bf16[2,256,384]{2,1,0:T(8,128)(2,1)} %tk_ref.3) | copy-start | bytes 1179652
  57.6 13.5 %copy-start.5 = (bf16[2,256,384]{2,1,0:T(8,128)(2,1)S(1)}, bf16[2,256,384]{2,1,0:T(8,128)(2,1)}, u32[]{:S(2)}) copy-start(bf16[2,256,384]{2,1,0:T(8,128)(2,1)} %tv_ref.3) | copy-start | bytes 1179652
  64.2 17.1 %collective-permute-start.7 = (bf16[384,768]{1,0:T(8,128)(2,1)S(1)}, bf16[384,768]{1,0:T(8,128)(2,1)S(1)}, u32[]{:S(2)}, u32[]{:S(2)}) collective-permute-start(bf16[384,768]{1,0:T(8,128)(2,1)S(1)} %get-tuple-element.44.own), channel_id=1, source_target_pairs={{0,8},{8,16},{16,24},{24,32},{32,40},{40,48},{48,56},{56,64},{64,7... | collective-permute-start | bytes 1769480 | tf_op jit(solution)/shard_map/ppermute | solution.py:44
  68.1 16.7 %collective-permute-start.8 = (bf16[384,768]{1,0:T(8,128)(2,1)S(1)}, bf16[384,768]{1,0:T(8,128)(2,1)S(1)}, u32[]{:S(2)}, u32[]{:S(2)}) collective-permute-start(bf16[384,768]{1,0:T(8,128)(2,1)S(1)} %get-tuple-element.44.own), channel_id=1, source_target_pairs={{8,0},{16,8},{24,16},{32,24},{40,32},{48,40},{56,48},{64,56},{72,6... | collective-permute-start | bytes 1769480 | tf_op jit(solution)/shard_map/ppermute | solution.py:44
  81.3 12.3 %copy-start.14 = (f32[384,768]{1,0:T(8,128)}, f32[384,768]{1,0:T(8,128)S(1)}, u32[]{:S(2)}) copy-start(f32[384,768]{1,0:T(8,128)S(1)} %get-tuple-element.60.down) | copy-start | bytes 3538948
  96.4 2.1 collective-permute-start.45
  101.1 9.9 %collective-permute-start.48 = (bf16[128,384]{1,0:T(8,128)(2,1)}, bf16[128,384]{1,0:T(8,128)(2,1)}, u32[]{:S(2)}, u32[]{:S(2)}) collective-permute-start(bf16[128,384]{1,0:T(8,128)(2,1)} %get-tuple-element.99), channel_id=1, source_target_pairs={{0,96},{8,104},{16,112},{24,120},{32,0},{40,8},{48,16},{56,24},{64... | collective-permute-start | bytes 294920 | tf_op jit(solution)/shard_map/ppermute | solution.py:39
  103.7 10.4 %collective-permute-start.47 = (bf16[128,384]{1,0:T(8,128)(2,1)}, bf16[128,384]{1,0:T(8,128)(2,1)}, u32[]{:S(2)}, u32[]{:S(2)}) collective-permute-start(bf16[128,384]{1,0:T(8,128)(2,1)} %get-tuple-element.100), channel_id=1, source_target_pairs={{0,32},{8,40},{16,48},{24,56},{32,64},{40,72},{48,80},{56,88},{64,... | collective-permute-start | bytes 294920 | tf_op jit(solution)/shard_map/ppermute | solution.py:39
  103.7 12.5 %collective-permute-start.46 = (bf16[128,384]{1,0:T(8,128)(2,1)}, bf16[128,384]{1,0:T(8,128)(2,1)}, u32[]{:S(2)}, u32[]{:S(2)}) collective-permute-start(bf16[128,384]{1,0:T(8,128)(2,1)} %get-tuple-element.98), channel_id=1, source_target_pairs={{0,64},{8,72},{16,80},{24,88},{32,96},{40,104},{48,112},{56,120},{... | collective-permute-start | bytes 294920 | tf_op jit(solution)/shard_map/ppermute | solution.py:39
  105.9 36.9 %collective-permute-start.27 = (bf16[384,768]{1,0:T(8,128)(2,1)}, bf16[384,768]{1,0:T(8,128)(2,1)}, u32[]{:S(2)}, u32[]{:S(2)}) collective-permute-start(bf16[384,768]{1,0:T(8,128)(2,1)} %get-tuple-element.61), channel_id=1, source_target_pairs={{0,8},{8,16},{16,24},{24,32},{32,40},{40,48},{48,56},{56,64},{64,7... | collective-permute-start | bytes 1769480 | tf_op jit(solution)/shard_map/ppermute | solution.py:44
  108.5 34.4 %collective-permute-start.28 = (bf16[384,768]{1,0:T(8,128)(2,1)}, bf16[384,768]{1,0:T(8,128)(2,1)}, u32[]{:S(2)}, u32[]{:S(2)}) collective-permute-start(bf16[384,768]{1,0:T(8,128)(2,1)} %get-tuple-element.62), channel_id=1, source_target_pairs={{8,0},{16,8},{24,16},{32,24},{40,32},{48,40},{56,48},{64,56},{72,6... | collective-permute-start | bytes 1769480 | tf_op jit(solution)/shard_map/ppermute | solution.py:44
  111.0 43.1 %collective-permute-start.9 = (bf16[384,768]{1,0:T(8,128)(2,1)S(1)}, bf16[384,768]{1,0:T(8,128)(2,1)}, u32[]{:S(2)}, u32[]{:S(2)}) collective-permute-start(bf16[384,768]{1,0:T(8,128)(2,1)S(1)} %get-tuple-element.47), channel_id=1, source_target_pairs={{0,8},{8,16},{16,24},{24,32},{32,40},{40,48},{48,56},{56,64},{64,7... | collective-permute-start | bytes 1769480 | tf_op jit(solution)/shard_map/ppermute | solution.py:44
  114.1 48.9 %collective-permute-start.10 = (bf16[384,768]{1,0:T(8,128)(2,1)S(1)}, bf16[384,768]{1,0:T(8,128)(2,1)}, u32[]{:S(2)}, u32[]{:S(2)}) collective-permute-start(bf16[384,768]{1,0:T(8,128)(2,1)S(1)} %get-tuple-element.48), channel_id=1, source_target_pairs={{8,0},{16,8},{24,16},{32,24},{40,32},{48,40},{56,48},{64,56},{72,6... | collective-permute-start | bytes 1769480 | tf_op jit(solution)/shard_map/ppermute | solution.py:44
  118.0 20.4 %collective-permute-start.49 = (bf16[128,384]{1,0:T(8,128)(2,1)}, bf16[128,384]{1,0:T(8,128)(2,1)}, u32[]{:S(2)}, u32[]{:S(2)}) collective-permute-start(bf16[128,384]{1,0:T(8,128)(2,1)} %fusion.3), channel_id=1, source_target_pairs={{0,16},{8,24},{16,0},{24,8},{32,48},{40,56},{48,32},{56,40},{64,80... | collective-permute-start | bytes 294920 | tf_op jit(solution)/shard_map/ppermute | solution.py:39
  138.4 55.2 %collective-permute-start.36 = (bf16[4,384,384]{2,1,0:T(8,128)(2,1)S(1)}, bf16[4,384,384]{2,1,0:T(8,128)(2,1)S(1)}, u32[]{:S(2)}, u32[]{:S(2)}) collective-permute-start(bf16[4,384,384]{2,1,0:T(8,128)(2,1)S(1)} %get-tuple-element.73), channel_id=1, source_target_pairs={{0,8},{8,0},{16,24},{24,16},{32,40},{40,32},{48,56},{56,48},{64,72... | collective-permute-start | bytes 3538952 | tf_op jit(solution)/shard_map/ppermute | solution.py:39
  142.8 54.0 %collective-permute-start.37 = (bf16[4,384,384]{2,1,0:T(8,128)(2,1)S(1)}, bf16[4,384,384]{2,1,0:T(8,128)(2,1)S(1)}, u32[]{:S(2)}, u32[]{:S(2)}) collective-permute-start(bf16[4,384,384]{2,1,0:T(8,128)(2,1)S(1)} %get-tuple-element.74), channel_id=1, source_target_pairs={{0,8},{8,0},{16,24},{24,16},{32,40},{40,32},{48,56},{56,48},{64,72... | collective-permute-start | bytes 3538952 | tf_op jit(solution)/shard_map/ppermute | solution.py:39
  142.8 28.0 %collective-permute-start.50 = (bf16[128,384]{1,0:T(8,128)(2,1)S(1)}, bf16[128,384]{1,0:T(8,128)(2,1)S(1)}, u32[]{:S(2)}, u32[]{:S(2)}) collective-permute-start(bf16[128,384]{1,0:T(8,128)(2,1)S(1)} %get-tuple-element.91), channel_id=1, source_target_pairs={{0,64},{8,72},{16,80},{24,88},{32,96},{40,104},{48,112},{56,120},{... | collective-permute-start | bytes 294920 | tf_op jit(solution)/shard_map/ppermute | solution.py:39
  148.8 16.9 %copy-start.13 = (f32[384,768]{1,0:T(8,128)S(1)}, f32[384,768]{1,0:T(8,128)}, u32[]{:S(2)}) copy-start(f32[384,768]{1,0:T(8,128)} %copy-done.12) | copy-start | bytes 3538948
  148.8 16.9 %copy-start.19 = (bf16[384,384]{1,0:T(8,128)(2,1)S(1)}, bf16[384,384]{1,0:T(8,128)(2,1)}, u32[]{:S(2)}) copy-start(bf16[384,384]{1,0:T(8,128)(2,1)} %copy-done.18) | copy-start | bytes 884740
  154.1 17.5 %collective-permute-start.51 = (bf16[128,384]{1,0:T(8,128)(2,1)S(1)}, bf16[128,384]{1,0:T(8,128)(2,1)S(1)}, u32[]{:S(2)}, u32[]{:S(2)}) collective-permute-start(bf16[128,384]{1,0:T(8,128)(2,1)S(1)} %get-tuple-element.91), channel_id=1, source_target_pairs={{0,32},{8,40},{16,48},{24,56},{32,64},{40,72},{48,80},{56,88},{64,... | collective-permute-start | bytes 294920 | tf_op jit(solution)/shard_map/ppermute | solution.py:39
  163.0 11.9 %collective-permute-start.52 = (bf16[128,384]{1,0:T(8,128)(2,1)S(1)}, bf16[128,384]{1,0:T(8,128)(2,1)S(1)}, u32[]{:S(2)}, u32[]{:S(2)}) collective-permute-start(bf16[128,384]{1,0:T(8,128)(2,1)S(1)} %get-tuple-element.91), channel_id=1, source_target_pairs={{0,96},{8,104},{16,112},{24,120},{32,0},{40,8},{48,16},{56,24},{64... | collective-permute-start | bytes 294920 | tf_op jit(solution)/shard_map/ppermute | solution.py:39
  170.9 8.5 %collective-permute-start.32 = (bf16[384,384]{1,0:T(8,128)(2,1)S(1)}, bf16[384,384]{1,0:T(8,128)(2,1)S(1)}, u32[]{:S(2)}, u32[]{:S(2)}) collective-permute-start(bf16[384,384]{1,0:T(8,128)(2,1)S(1)} %get-tuple-element.69), channel_id=1, source_target_pairs={{0,1},{1,2},{2,3},{3,0},{4,5},{5,6},{6,7},{7,4},{8,9},{9,10},{10,1... | collective-permute-start | bytes 884744 | tf_op jit(solution)/shard_map/ppermute | solution.py:32
  171.6 11.8 %collective-permute-start.30 = (bf16[384,384]{1,0:T(8,128)(2,1)S(1)}, bf16[384,384]{1,0:T(8,128)(2,1)S(1)}, u32[]{:S(2)}, u32[]{:S(2)}) collective-permute-start(bf16[384,384]{1,0:T(8,128)(2,1)S(1)} %get-tuple-element.66), channel_id=1, source_target_pairs={{0,3},{1,0},{2,1},{3,2},{4,7},{5,4},{6,5},{7,6},{8,11},{9,8},{10,9... | collective-permute-start | bytes 884744 | tf_op jit(solution)/shard_map/ppermute | solution.py:32
  174.9 10.8 %collective-permute-start.14 = (bf16[384,384]{1,0:T(8,128)(2,1)S(1)}, bf16[384,384]{1,0:T(8,128)(2,1)S(1)}, u32[]{:S(2)}, u32[]{:S(2)}) collective-permute-start(bf16[384,384]{1,0:T(8,128)(2,1)S(1)} %get-tuple-element.55), channel_id=1, source_target_pairs={{0,1},{1,2},{2,3},{3,0},{4,5},{5,6},{6,7},{7,4},{8,9},{9,10},{10,1... | collective-permute-start | bytes 884744 | tf_op jit(solution)/shard_map/ppermute | solution.py:32
  179.4 17.7 %collective-permute-start.38 = (bf16[384,1152]{1,0:T(8,128)(2,1)S(1)}, bf16[384,1152]{1,0:T(8,128)(2,1)S(1)}, u32[]{:S(2)}, u32[]{:S(2)}) collective-permute-start(bf16[384,1152]{1,0:T(8,128)(2,1)S(1)} %get-tuple-element.75.g0), channel_id=1, source_target_pairs={{0,8},{8,0},{16,24},{24,16},{32,40},{40,32},{48,56},{56,48},{64,72... | collective-permute-start | bytes 2654216 | tf_op jit(solution)/shard_map/ppermute | solution.py:39
  183.4 13.7 %collective-permute-start.39 = (bf16[384,1152]{1,0:T(8,128)(2,1)S(1)}, bf16[384,1152]{1,0:T(8,128)(2,1)S(1)}, u32[]{:S(2)}, u32[]{:S(2)}) collective-permute-start(bf16[384,1152]{1,0:T(8,128)(2,1)S(1)} %get-tuple-element.76.g1), channel_id=1, source_target_pairs={{0,8},{8,0},{16,24},{24,16},{32,40},{40,32},{48,56},{56,48},{64,72... | collective-permute-start | bytes 2654216 | tf_op jit(solution)/shard_map/ppermute | solution.py:39
  185.7 6.3 %collective-permute-start.12 = (bf16[384,384]{1,0:T(8,128)(2,1)S(1)}, bf16[384,384]{1,0:T(8,128)(2,1)S(1)}, u32[]{:S(2)}, u32[]{:S(2)}) collective-permute-start(bf16[384,384]{1,0:T(8,128)(2,1)S(1)} %get-tuple-element.52), channel_id=1, source_target_pairs={{0,3},{1,0},{2,1},{3,2},{4,7},{5,4},{6,5},{7,6},{8,11},{9,8},{10,9... | collective-permute-start | bytes 884744 | tf_op jit(solution)/shard_map/ppermute | solution.py:32
  192.0 19.0 %collective-permute-start.34 = (bf16[384,384]{1,0:T(8,128)(2,1)S(1)}, bf16[384,384]{1,0:T(8,128)(2,1)S(1)}, u32[]{:S(2)}, u32[]{:S(2)}) collective-permute-start(bf16[384,384]{1,0:T(8,128)(2,1)S(1)} %get-tuple-element.70), channel_id=1, source_target_pairs={{0,3},{1,0},{2,1},{3,2},{4,7},{5,4},{6,5},{7,6},{8,11},{9,8},{10,9... | collective-permute-start | bytes 884744 | tf_op jit(solution)/shard_map/ppermute | solution.py:32
  193.6 15.0 %collective-permute-start.53 = (bf16[2,256,384]{2,1,0:T(8,128)(2,1)}, bf16[2,256,384]{2,1,0:T(8,128)(2,1)S(1)}, u32[]{:S(2)}, u32[]{:S(2)}) collective-permute-start(bf16[2,256,384]{2,1,0:T(8,128)(2,1)} %bitcast.27), channel_id=1, source_target_pairs={{0,8},{8,0},{16,24},{24,16},{32,40},{40,32},{48,56},{56,48},{64,72... | collective-permute-start | bytes 1179656 | tf_op jit(solution)/shard_map/ppermute | solution.py:39
  196.8 16.6 %collective-permute-start.33 = (bf16[384,384]{1,0:T(8,128)(2,1)S(1)}, bf16[384,384]{1,0:T(8,128)(2,1)S(1)}, u32[]{:S(2)}, u32[]{:S(2)}) collective-permute-start(bf16[384,384]{1,0:T(8,128)(2,1)S(1)} %add_convert_fusion.4), channel_id=1, source_target_pairs={{0,1},{1,2},{2,3},{3,0},{4,5},{5,6},{6,7},{7,4},{8,9},{9,10},{10,1... | collective-permute-start | bytes 884744 | tf_op jit(solution)/shard_map/ppermute | solution.py:32
  207.1 21.1 %collective-permute-start.42 = (bf16[384,1152]{1,0:T(8,128)(2,1)S(1)}, bf16[384,1152]{1,0:T(8,128)(2,1)S(1)}, u32[]{:S(2)}, u32[]{:S(2)}) collective-permute-start(bf16[384,1152]{1,0:T(8,128)(2,1)S(1)} %get-tuple-element.80), channel_id=1, source_target_pairs={{0,96},{8,104},{16,112},{24,120},{32,0},{40,8},{48,16},{56,24},{64... | collective-permute-start | bytes 2654216 | tf_op jit(solution)/shard_map/ppermute | solution.py:39
  207.5 22.8 %collective-permute-start.41 = (bf16[384,1152]{1,0:T(8,128)(2,1)S(1)}, bf16[384,1152]{1,0:T(8,128)(2,1)S(1)}, u32[]{:S(2)}, u32[]{:S(2)}) collective-permute-start(bf16[384,1152]{1,0:T(8,128)(2,1)S(1)} %get-tuple-element.79), channel_id=1, source_target_pairs={{0,32},{8,40},{16,48},{24,56},{32,64},{40,72},{48,80},{56,88},{64,... | collective-permute-start | bytes 2654216 | tf_op jit(solution)/shard_map/ppermute | solution.py:39
  208.6 39.3 %collective-permute-start.40 = (bf16[384,1152]{1,0:T(8,128)(2,1)S(1)}, bf16[384,1152]{1,0:T(8,128)(2,1)S(1)}, u32[]{:S(2)}, u32[]{:S(2)}) collective-permute-start(bf16[384,1152]{1,0:T(8,128)(2,1)S(1)} %get-tuple-element.78), channel_id=1, source_target_pairs={{0,64},{8,72},{16,80},{24,88},{32,96},{40,104},{48,112},{56,120},{... | collective-permute-start | bytes 2654216 | tf_op jit(solution)/shard_map/ppermute | solution.py:39
  211.1 7.5 %collective-permute-start.16 = (bf16[384,384]{1,0:T(8,128)(2,1)S(1)}, bf16[384,384]{1,0:T(8,128)(2,1)S(1)}, u32[]{:S(2)}, u32[]{:S(2)}) collective-permute-start(bf16[384,384]{1,0:T(8,128)(2,1)S(1)} %get-tuple-element.56), channel_id=1, source_target_pairs={{0,3},{1,0},{2,1},{3,2},{4,7},{5,4},{6,5},{7,6},{8,11},{9,8},{10,9... | collective-permute-start | bytes 884744 | tf_op jit(solution)/shard_map/ppermute | solution.py:32
  213.4 8.2 %collective-permute-start.15 = (bf16[384,384]{1,0:T(8,128)(2,1)S(1)}, bf16[384,384]{1,0:T(8,128)(2,1)S(1)}, u32[]{:S(2)}, u32[]{:S(2)}) collective-permute-start(bf16[384,384]{1,0:T(8,128)(2,1)S(1)} %add_convert_fusion.8), channel_id=1, source_target_pairs={{0,1},{1,2},{2,3},{3,0},{4,5},{5,6},{6,7},{7,4},{8,9},{9,10},{10,1... | collective-permute-start | bytes 884744 | tf_op jit(solution)/shard_map/ppermute | solution.py:32
  218.5 31.6 %collective-permute-start.29 = (bf16[384,384]{1,0:T(8,128)(2,1)S(1)}, bf16[384,384]{1,0:T(8,128)(2,1)S(1)}, u32[]{:S(2)}, u32[]{:S(2)}) collective-permute-start(bf16[384,384]{1,0:T(8,128)(2,1)S(1)} %get-tuple-element.64), channel_id=1, source_target_pairs={{0,1},{1,2},{2,3},{3,0},{4,5},{5,6},{6,7},{7,4},{8,9},{9,10},{10,1... | collective-permute-start | bytes 884744 | tf_op jit(solution)/shard_map/ppermute | solution.py:32
  221.6 41.7 %collective-permute-start.11 = (bf16[384,384]{1,0:T(8,128)(2,1)S(1)}, bf16[384,384]{1,0:T(8,128)(2,1)S(1)}, u32[]{:S(2)}, u32[]{:S(2)}) collective-permute-start(bf16[384,384]{1,0:T(8,128)(2,1)S(1)} %get-tuple-element.50), channel_id=1, source_target_pairs={{0,1},{1,2},{2,3},{3,0},{4,5},{5,6},{6,7},{7,4},{8,9},{9,10},{10,1... | collective-permute-start | bytes 884744 | tf_op jit(solution)/shard_map/ppermute | solution.py:32
  228.2 23.4 %collective-permute-start.31 = (bf16[384,384]{1,0:T(8,128)(2,1)S(1)}, bf16[384,384]{1,0:T(8,128)(2,1)S(1)}, u32[]{:S(2)}, u32[]{:S(2)}) collective-permute-start(bf16[384,384]{1,0:T(8,128)(2,1)S(1)} %add_convert_fusion.5), channel_id=1, source_target_pairs={{0,3},{1,0},{2,1},{3,2},{4,7},{5,4},{6,5},{7,6},{8,11},{9,8},{10,9... | collective-permute-start | bytes 884744 | tf_op jit(solution)/shard_map/ppermute | solution.py:32
  230.3 33.0 %collective-permute-start.13 = (bf16[384,384]{1,0:T(8,128)(2,1)S(1)}, bf16[384,384]{1,0:T(8,128)(2,1)S(1)}, u32[]{:S(2)}, u32[]{:S(2)}) collective-permute-start(bf16[384,384]{1,0:T(8,128)(2,1)S(1)} %add_convert_fusion.9), channel_id=1, source_target_pairs={{0,3},{1,0},{2,1},{3,2},{4,7},{5,4},{6,5},{7,6},{8,11},{9,8},{10,9... | collective-permute-start | bytes 884744 | tf_op jit(solution)/shard_map/ppermute | solution.py:32
  248.0 7.1 %collective-permute-start.35 = (bf16[384,384]{1,0:T(8,128)(2,1)S(1)}, bf16[384,384]{1,0:T(8,128)(2,1)S(1)}, u32[]{:S(2)}, u32[]{:S(2)}) collective-permute-start(bf16[384,384]{1,0:T(8,128)(2,1)S(1)} %add_convert_fusion.3), channel_id=1, source_target_pairs={{0,4},{1,5},{2,6},{3,7},{4,0},{5,1},{6,2},{7,3},{8,12},{9,13},{10,... | collective-permute-start | bytes 884744 | tf_op jit(solution)/shard_map/ppermute | solution.py:32
  250.1 13.2 %collective-permute-start.17 = (bf16[384,384]{1,0:T(8,128)(2,1)S(1)}, bf16[384,384]{1,0:T(8,128)(2,1)S(1)}, u32[]{:S(2)}, u32[]{:S(2)}) collective-permute-start(bf16[384,384]{1,0:T(8,128)(2,1)S(1)} %add_convert_fusion.7), channel_id=1, source_target_pairs={{0,4},{1,5},{2,6},{3,7},{4,0},{5,1},{6,2},{7,3},{8,12},{9,13},{10,... | collective-permute-start | bytes 884744 | tf_op jit(solution)/shard_map/ppermute | solution.py:32
  251.5 15.7 %collective-permute-start.44 = (bf16[192,1152]{1,0:T(8,128)(2,1)S(1)}, bf16[192,1152]{1,0:T(8,128)(2,1)S(1)}, u32[]{:S(2)}, u32[]{:S(2)}) collective-permute-start(bf16[192,1152]{1,0:T(8,128)(2,1)S(1)} %get-tuple-element.93), channel_id=1, source_target_pairs={{0,8},{8,24},{16,0},{24,16},{32,40},{40,56},{48,32},{56,48},{64,72... | collective-permute-start | bytes 1327112 | tf_op jit(solution)/shard_map/ppermute | solution.py:269
  255.0 17.2 %collective-permute-start.43 = (bf16[192,1152]{1,0:T(8,128)(2,1)S(1)}, bf16[192,1152]{1,0:T(8,128)(2,1)S(1)}, u32[]{:S(2)}, u32[]{:S(2)}) collective-permute-start(bf16[192,1152]{1,0:T(8,128)(2,1)S(1)} %get-tuple-element.92), channel_id=1, source_target_pairs={{8,16},{16,8},{40,48},{48,40},{72,80},{80,72},{104,112},{112,104},... | collective-permute-start | bytes 1327112 | tf_op jit(solution)/shard_map/ppermute | solution.py:270
  (20 other events, 25.5 us)
